TPU v7x, 256 devices: a whole 4x4x8 slice. The times are simulated.
256 devices in a mesh: seq: 64 (over y_lo, z, x), head: 4 (over y_hi, core).
Axes of the slice: x: 4, y: 4 (y_hi: 2, y_lo: 2; y = y_hi * 2 + y_lo), z: 8, core: 2. Of those that a mesh axis runs over, the one named last changes fastest.
Arguments:
- tokens: bfloat16 [24576, 1280], P('seq'), may hold values from -20 to 20
- w_qkv: bfloat16 [1280, 3, 1280], P(None, None, 'head'), may hold values from -0.15625 to 0.15625
- w_out: bfloat16 [1280, 1280], P('head'), may hold values from -0.15625 to 0.15625
- cotangent: bfloat16 [24576, 1280], P('seq'), may hold values from -16 to 16
- block_mask: int32 [192, 192], P('seq'), may hold values from 0 to 1, as said below
- regions: int32 [24576], P('seq'), may hold values from 0 to 3
Outputs:
- mixed: bfloat16 [24576, 1280], P('seq', 'head')
- grad_tokens: bfloat16 [24576, 1280], P('seq', 'head')
- grad_qkv: float32 [1280, 3, 1280], P('seq', None, 'head')
- grad_out: float32 [1280, 1280], P('head', 'seq')
Inputs may be any that keep to these rules, and one draw needn't show every extreme that they name: block_mask is 0 for every block pair whose token ranges of 384 lie more than 3 ranges apart on the closed loop of ranges; pairs exactly 3 ranges apart are 1 in some block of every range.
All inputs are finite; a program needn't handle non-finite values.
Results may differ from a plain program's by a relative error of at most 0.02.
Values may be sent and summed in bfloat16 or wider, within the bound.
No kernel may reach another device: no remote copies, remote signals or barrier semaphores. Data moves between devices by JAX's collectives and lax.ppermute only.
A program may use at most 128 MiB of HBM per device.

v0:
```python
import functools

import jax
import jax.numpy as jnp
from jax import lax
from jax.experimental import pallas as pl
from jax.experimental.pallas import tpu as pltpu
from jax.sharding import Mesh
from jax.sharding import PartitionSpec as P

HD = 80
BLOCK = 128
SPAN = 3
TOK = 384
GROUP = 4
PIECES = GROUP + 2 * SPAN
WINDOW = 2 * SPAN + 1
ROW = GROUP * TOK
HALO = SPAN * TOK
KEYS = PIECES * TOK
ROWS = 16
NB = 192
SCALE = HD ** (-0.5)
LOG2E = 1.4426950408889634
NEG = -1e30
BF = jnp.bfloat16
F32 = jnp.float32
MIB = 1024 * 1024
SENT = 4 * HD + 16
ROW_AXES = ("y", "z")
SEQ_AXES = ("y", "z", "x")
HEAD_AXES = ("h", "c")


def shift(value, axis, steps):
    count = lax.axis_size(axis)
    return lax.ppermute(value, axis, [(i, (i + steps) % count) for i in range(count)])


def spec_vmem():
    return pl.BlockSpec(memory_space=pltpu.VMEM)


def spec_smem():
    return pl.BlockSpec(memory_space=pltpu.SMEM)


def call(kernel, outs, ins, scratch=(), mib=12, flops=0, moved=0, exps=0, spaces=None, out_spaces=None):
    anywhere = pl.BlockSpec(memory_space=pl.ANY)
    spec = {"v": spec_vmem(), "s": spec_smem(), "a": anywhere, "h": anywhere, "f": spec_vmem()}
    kept = {"h": pltpu.HBM, "f": pltpu.VMEM}
    spaces = spaces or "s" + "v" * (len(ins) - 1)
    out_spaces = out_spaces or "v" * len(outs)
    ins = [pltpu.with_memory_space_constraint(a, kept[c]) if c in kept else a for a, c in zip(ins, spaces)]
    return pl.pallas_call(
        kernel,
        out_shape=[kept.get(c, jax.ShapeDtypeStruct)(s, d) for (s, d), c in zip(outs, out_spaces)],
        in_specs=[spec[c] for c in spaces],
        out_specs=[spec[c] for c in out_spaces],
        scratch_shapes=list(scratch),
        compiler_params=pltpu.CompilerParams(vmem_limit_bytes=mib * MIB),
        cost_estimate=pl.CostEstimate(flops=flops, bytes_accessed=moved, transcendentals=exps),
    )(*ins)


def dot_nn(a, b):
    return lax.dot_general(a, b, (((1,), (0,)), ((), ())), preferred_element_type=F32)


def dot_nt(a, b):
    return lax.dot_general(a, b, (((1,), (1,)), ((), ())), preferred_element_type=F32)


def project_kernel(place, w, tokens, w_out, cotangent, regions, mask, o0, o1, o2, o3, parts,
                   wv, tv, wov, cv, rv, mv, extra, held, stage, sems):
    x = place[1]
    half = tokens.shape[0] // 2
    mine = pl.ds(pl.multiple_of(place[3] * half, half), half)
    pairs = ((w, wv), (tokens, tv), (w_out, wov), (cotangent, cv), (regions, rv), (mask, mv))
    copies = [pltpu.make_async_copy(a, b, sems.at[n]) for n, (a, b) in enumerate(pairs)]
    for n in (1, 0, 3, 2, 4, 5):
        copies[n].start()
    copies[4].wait()
    copies[5].wait()
    extra[...] = jnp.zeros_like(extra)
    extra[0:1, :] = rv[...].reshape(1, -1).astype(F32)
    extra[1:4, :NB] = mv[...].astype(F32)
    copies[1].wait()
    copies[0].wait()
    width = tokens.shape[0]
    held[:3] = dot_nt(wv[...], tv[...]).astype(BF).reshape(3, GROUP, HD, width)
    copies[3].wait()
    copies[2].wait()
    held[3] = dot_nt(wov[...], cv[...]).astype(BF).reshape(GROUP, HD, width)
    outs = []
    for k, out in enumerate((o0, o1, o2, o3)):
        head = lax.rem(x + k, GROUP)
        for piece in range(3):
            stage[k, piece * HD : (piece + 1) * HD, :] = held[piece, head]
        stage[k, 3 * HD : 3 * HD + 16, :] = extra[...].astype(BF)
        stage[k, 3 * HD + 16 :, :] = held[3, head]
        outs.append(pltpu.make_async_copy(stage.at[k], out, sems.at[6 + k]))
    outs.append(pltpu.make_async_copy(tv.at[mine], parts.at[0], sems.at[10]))
    outs.append(pltpu.make_async_copy(cv.at[mine], parts.at[1], sems.at[11]))
    for copy in outs:
        copy.start()
    for copy in outs:
        copy.wait()


def ready_kernel(place, r0, r1, r2, r3, w, w_out, wt, w_out_t, eff, qn, don):
    row = place[0]
    x = place[1]
    block_of = lax.broadcasted_iota(jnp.int32, (256, KEYS), 1) // BLOCK
    block_id = lax.rem(block_of + row * (ROW // BLOCK) - HALO // BLOCK + NB, NB)
    pick = jnp.where(block_id == lax.broadcasted_iota(jnp.int32, (256, KEYS), 0), 1.0, 0.0).astype(BF)
    for k, ref in enumerate((r0, r1, r2, r3)):
        pos = lax.rem(x - k + GROUP, GROUP)
        eff[pos] = dot_nn(ref[3 * HD : 3 * HD + 16, :256], pick)
        qn[pos] = ref[:HD, :].astype(F32).T.astype(BF)
        don[pos] = ref[3 * HD + 16 :, :].astype(F32).T
    wt[...] = w[...].T
    w_out_t[...] = w_out[...].T


def halo_kernel(place, r0, r1, r2, r3, to_next, to_prev):
    x = place[1]
    for k, ref in enumerate((r0, r1, r2, r3)):
        pos = lax.rem(x - k + GROUP, GROUP)

        @pl.when(pos >= 1)
        def _():
            at = pl.multiple_of((pos - 1) * TOK, TOK)
            to_next[:, pl.ds(at, TOK)] = ref[HD : 3 * HD + 16, :]

        @pl.when(pos <= 2)
        def _():
            at = pl.multiple_of(pos * TOK, TOK)
            to_prev[:, pl.ds(at, TOK)] = ref[HD : 3 * HD + 16, :]


def attention_kernel(place, r0, r1, r2, r3, eff, qn, don, from_prev, from_next,
                     early, gp, gn, own, o0, o1, o2, o3,
                     kt, vt, reg, qt, s_ref, p_ref, ds_ref, dk, dv):
    x = place[1]
    kt[:, :HALO] = from_prev[:HD, :]
    vt[:, :HALO] = from_prev[HD : 2 * HD, :]
    reg[:, :HALO] = from_prev[2 * HD :, :].astype(F32)
    kt[:, HALO + ROW :] = from_next[:HD, :]
    vt[:, HALO + ROW :] = from_next[HD : 2 * HD, :]
    reg[:, HALO + ROW :] = from_next[2 * HD :, :].astype(F32)
    for k, ref in enumerate((r0, r1, r2, r3)):
        pos = lax.rem(x - k + GROUP, GROUP)
        at = pl.multiple_of(HALO + pos * TOK, TOK)
        kt[:, pl.ds(at, TOK)] = ref[HD : 2 * HD, :]
        vt[:, pl.ds(at, TOK)] = ref[2 * HD : 3 * HD, :]
        reg[:, pl.ds(at, TOK)] = ref[3 * HD : 3 * HD + 16, :].astype(F32)
        qt[pos] = ref[:HD, :]
    dk[...] = jnp.zeros_like(dk)
    dv[...] = jnp.zeros_like(dv)

    def step(r, carry):
        at = pl.multiple_of(r * TOK, TOK)

        def win(c):
            return pl.ds(pl.multiple_of(at + c * TOK, TOK), TOK)

        q_n = qn[r]
        do_n = don[r]
        reg_q = reg[:, pl.ds(pl.multiple_of(HALO + at, TOK), TOK)].T[:, 0:1]
        top = [jnp.full((BLOCK, BLOCK), NEG, F32)] * 3
        for c in range(WINDOW):
            raw = dot_nn(q_n, kt[:, win(c)])
            key_reg = reg[0:1, win(c)]
            blocks = lax.broadcasted_iota(jnp.int32, (1, TOK), 1) // BLOCK
            for i in range(3):
                open_ = eff[r, 1 + i : 2 + i, win(c)] > 0.5
                if c == SPAN:
                    open_ = open_ | (blocks == i)
                key_eff = jnp.where(open_, key_reg, -1.0)
                rows = slice(i * BLOCK, (i + 1) * BLOCK)
                s = jnp.where(reg_q[rows] == key_eff, raw[rows], NEG)
                s_ref[rows, c * TOK : (c + 1) * TOK] = s
                for g in range(3):
                    top[i] = jnp.maximum(top[i], s[:, g * BLOCK : (g + 1) * BLOCK])
        m = jnp.concatenate([jnp.max(t, axis=1, keepdims=True) for t in top], axis=0)
        total = jnp.zeros((TOK, BLOCK), F32)
        out = jnp.zeros((TOK, HD), F32)
        for c in range(WINDOW):
            p = jnp.exp2((s_ref[:, c * TOK : (c + 1) * TOK] - m) * (SCALE * LOG2E))
            for g in range(3):
                total = total + p[:, g * BLOCK : (g + 1) * BLOCK]
            pb = p.astype(BF)
            p_ref[:, c * TOK : (c + 1) * TOK] = pb
            out = out + dot_nt(pb, vt[:, win(c)])
        inv = 1.0 / jnp.sum(total, axis=1, keepdims=True)
        at_n = (out * inv).astype(BF).astype(F32)
        dos_n = (do_n * (inv * SCALE)).astype(BF)
        delta = jnp.sum(dos_n.astype(F32) * at_n, axis=1, keepdims=True)
        d_q = jnp.zeros((TOK, HD), F32)
        for c in range(WINDOW):
            cols = slice(c * TOK, (c + 1) * TOK)
            dp = dot_nn(dos_n, vt[:, win(c)])
            ds = (p_ref[:, cols].astype(F32) * (dp - delta)).astype(BF)
            ds_ref[:, cols] = ds
            d_q = d_q + dot_nt(ds, kt[:, win(c)])
        dos_t = dos_n.astype(F32).T.astype(BF)
        for c in range(WINDOW):
            cols = slice(c * TOK, (c + 1) * TOK)
            dk[:, win(c)] += dot_nn(qt[r], ds_ref[:, cols])
            dv[:, win(c)] += dot_nn(dos_t, p_ref[:, cols])
        attn_t = at_n.T.astype(BF)
        dq_t = d_q.T.astype(BF)
        both = jnp.concatenate([attn_t, dq_t], axis=0)
        early[:, pl.ds(at, TOK)] = both
        k_to = lax.rem(r - x + GROUP, GROUP)
        for k, out_k in enumerate((o0, o1, o2, o3)):
            @pl.when(k_to == k)
            def _():
                out_k[...] = both
        return carry

    lax.fori_loop(0, GROUP, step, 0)
    unscale = 1.0 / SCALE
    gp[:HD, :] = dk[:, :HALO].astype(BF)
    gp[HD:, :] = (dv[:, :HALO] * unscale).astype(BF)
    gn[:HD, :] = dk[:, HALO + ROW :].astype(BF)
    gn[HD:, :] = (dv[:, HALO + ROW :] * unscale).astype(BF)
    own[:HD, :] = dk[:, HALO : HALO + ROW]
    own[HD:, :] = dv[:, HALO : HALO + ROW] * unscale


def attention(place, parts, ready, from_prev, from_next):
    chunk = ((2 * HD, TOK), BF)
    outs = [((2 * HD, ROW), BF)] + [((2 * HD, HALO), BF)] * 2 + [((2 * HD, ROW), F32)] + [chunk] * 4
    scratch = [
        pltpu.VMEM((HD, KEYS), BF),
        pltpu.VMEM((HD, KEYS), BF),
        pltpu.VMEM((16, KEYS), F32),
        pltpu.VMEM((GROUP, HD, TOK), BF),
        pltpu.VMEM((TOK, WINDOW * TOK), F32),
        pltpu.VMEM((TOK, WINDOW * TOK), BF),
        pltpu.VMEM((TOK, WINDOW * TOK), BF),
        pltpu.VMEM((HD, KEYS), F32),
        pltpu.VMEM((HD, KEYS), F32),
    ]
    return call(
        attention_kernel, outs, [place, *parts, *ready, from_prev, from_next], scratch, mib=28, out_spaces="f" * len(outs),
        flops=12 * ROW * WINDOW * TOK * 128, moved=6_000_000, exps=ROW * WINDOW * TOK,
    )


def combine_kernel(place, own, from_next, from_prev, full, c0, c1, c2, c3):
    x = place[1]
    full[:, :TOK] = (own[:, :TOK] + from_prev[:, :TOK].astype(F32)).astype(BF)
    middle = own[:, TOK:HALO] + from_next[:, : HALO - TOK].astype(F32)
    full[:, TOK:HALO] = (middle + from_prev[:, TOK:].astype(F32)).astype(BF)
    full[:, HALO:] = (own[:, HALO:] + from_next[:, HALO - TOK :].astype(F32)).astype(BF)
    for k, out in enumerate((c0, c1, c2, c3)):
        at = pl.multiple_of(lax.rem(x + k, GROUP) * TOK, TOK)
        out[...] = full[:, pl.ds(at, TOK)]


def early_kernel(scale, place, values, gathered, out, tokens, cotangent, sems):
    count, _, rows, _ = gathered.shape
    copies = []
    for which, into in ((1, cotangent), (0, tokens)):
        for n in range(count):
            sem = sems.at[which, n]
            copies.append(pltpu.make_async_copy(gathered.at[n, which], into.at[n * rows : (n + 1) * rows], sem))
    for copy in copies:
        copy.start()
    for copy in copies[:count]:
        copy.wait()
    out[:HD, :] = dot_nn(values[:HD, :], cotangent[...]) * scale
    for copy in copies[count:]:
        copy.wait()
    out[HD:, :] = dot_nn(values[HD:, :], tokens[...]) * scale


def late_kernel(scale, place, early, values, tokens, send, keep):
    half = early.shape[1] // 2
    y = place[2]
    for other, out in ((1, send), (0, keep)):
        cols = pl.ds(pl.multiple_of(lax.rem(y + other, 2) * half, half), half)
        out[: 2 * HD, :] = early[:, cols].astype(out.dtype)
        out[2 * HD :, :] = (dot_nn(values[...], tokens[:, cols]) * scale).astype(out.dtype)


def sum_turn_kernel(place, keep, got, out):
    out[...] = (keep[...] + got[...].astype(F32)).T.astype(BF)


def share_kernel(place, *refs):
    ins, (w_out_t, wt, send, keep, attn, grads) = refs[: 2 * GROUP], refs[2 * GROUP :]
    x = place[1]
    core = place[3]
    for k in range(GROUP):
        head = lax.rem(x - k + GROUP, GROUP)
        attn[head] = ins[k][:HD, :]
        grads[0, head] = ins[k][HD:, :]
        grads[1, head] = ins[GROUP + k][:HD, :]
        grads[2, head] = ins[GROUP + k][HD:, :]
    local = GROUP * HD
    for n, (weights, held) in enumerate(((w_out_t, attn), (wt, grads))):
        values = held[...].reshape(-1, TOK)
        for other, out in ((1, send), (0, keep)):
            for h in range(2):
                at = pl.multiple_of((2 * h + lax.rem(core + other, 2)) * local, local)
                out[n, h] = dot_nn(weights[pl.ds(at, local), :], values).astype(out.dtype)


def core_sum_kernel(place, keep, got, other, mine):
    h = place[4]
    for n in range(2):
        other[n] = (keep[n, 1 - h] + got[n, 1 - h].astype(F32)).astype(BF)
        mine[n] = keep[n, h] + got[n, h].astype(F32)


def head_sum_kernel(place, mine, got, mixed, grad):
    mixed[...] = (mine[0] + got[0].astype(F32)).astype(BF)
    grad[...] = (mine[1] + got[1].astype(F32)).astype(BF)


def scatter_core(place, values, w_out_t, wt):
    local = w_out_t.shape[1]
    model = w_out_t.shape[0]
    shape = (2, 2, local, TOK)
    send, keep = call(
        share_kernel,
        [(shape, BF), (shape, F32)],
        [place, *values, w_out_t, wt],
        [pltpu.VMEM((GROUP, HD, TOK), BF), pltpu.VMEM((3, GROUP, HD, TOK), BF)],
        mib=14, out_spaces="ff",
    )
    got = shift(send, "c", 1)
    return call(
        core_sum_kernel, [((2, local, TOK), BF), ((2, local, TOK), F32)], [place, keep, got],
        out_spaces="ff",
    )


def on_device(tokens, w_qkv, w_out, cotangent, block_mask, regions):
    width, model = tokens.shape
    local = w_out.shape[0]
    x = lax.axis_index("x")
    y = lax.axis_index("y")
    row = y * (ROWS // 2) + lax.axis_index("z")
    place = jnp.stack([row, x, y, lax.axis_index("c"), lax.axis_index("h")]).astype(jnp.int32)
    grad_scale = (width * lax.axis_size(SEQ_AXES)) ** (-0.5)
    w2 = w_qkv.transpose(1, 2, 0).reshape(3 * local, model)

    *sent, parts_mine = call(
        project_kernel,
        [((SENT, width), BF)] * GROUP + [((2, width // 2, model), BF)],
        [place, w2, tokens, w_out, cotangent, regions, block_mask],
        [
            pltpu.VMEM((3 * local, model), BF),
            pltpu.VMEM((width, model), BF),
            pltpu.VMEM((local, model), BF),
            pltpu.VMEM((width, model), BF),
            pltpu.VMEM(regions.shape, jnp.int32),
            pltpu.VMEM(block_mask.shape, jnp.int32),
            pltpu.VMEM((16, width), F32),
            pltpu.VMEM((4, GROUP, HD, width), BF),
            pltpu.VMEM((GROUP, SENT, width), BF),
            pltpu.SemaphoreType.DMA((12,)),
        ],
        mib=16, spaces="shhhhhh", out_spaces="hhhhh",
        flops=2 * 4 * local * model * width, moved=8_000_000,
    )
    parts = [sent[0]] + [shift(sent[k], "x", k) for k in (1, 2, 3)]
    gathered = lax.all_gather(parts_mine, ("x", "c"), axis=0)
    to_next, to_prev = call(
        halo_kernel, [((2 * HD + 16, HALO), BF)] * 2, [place, *parts], moved=2_000_000
    )
    from_prev = shift(to_next, ROW_AXES, 1)
    from_next = shift(to_prev, ROW_AXES, -1)
    w_late, _ = lax.optimization_barrier((w2, to_next))
    w_t, w_out_t, *ready = call(
        ready_kernel,
        [
            ((model, 3 * local), BF), ((model, local), BF),
            ((GROUP, 16, KEYS), F32), ((GROUP, width, HD), BF), ((GROUP, width, HD), F32),
        ],
        [place, *parts, w_late, w_out], moved=8_000_000, mib=20,
    )
    from_prev, from_next, ready = lax.optimization_barrier((from_prev, from_next, ready))

    early, gp, gn, own, *mine = attention(place, parts, ready, from_prev, from_next)
    back_next = shift(gp, ROW_AXES, -1)
    back_prev = shift(gn, ROW_AXES, 1)
    aq_all = [mine[0]] + [shift(mine[k], "x", k) for k in (1, 2, 3)]
    early_w, tokens_row = call(
        functools.partial(early_kernel, grad_scale),
        [((2 * HD, model), F32), ((ROW, model), BF)],
        [place, early, gathered],
        [pltpu.VMEM((ROW, model), BF), pltpu.SemaphoreType.DMA((2, 2 * GROUP))],
        spaces="svh", out_spaces="ff", mib=16,
    )
    back_next, back_prev, early_w = lax.optimization_barrier((back_next, back_prev, early_w))

    dkv, *kv_chunks = call(
        combine_kernel, [((2 * HD, ROW), BF)] + [((2 * HD, width), BF)] * GROUP,
        [place, own, back_next, back_prev], out_spaces="f" * 5,
    )
    kv_all = [kv_chunks[0]] + [shift(kv_chunks[k], "x", k) for k in (1, 2, 3)]
    send_w, keep_w = call(
        functools.partial(late_kernel, grad_scale),
        [((4 * HD, model // 2), BF), ((4 * HD, model // 2), F32)],
        [place, early_w, dkv, tokens_row], out_spaces="ff",
    )
    send_w, kv_all = lax.optimization_barrier((send_w, kv_all))
    got_w = shift(send_w, "y", 1)
    other, mine = scatter_core(place, [*aq_all, *kv_all], w_out_t, w_t)

    got_w, other = lax.optimization_barrier((got_w, other))
    got = shift(other, "h", 1)
    (half_w,) = call(
        sum_turn_kernel, [((model // 2, 4 * HD), BF)], [place, keep_w, got_w]
    )
    spread = lax.all_to_all(half_w.reshape(ROWS // 2, model // ROWS, 4 * HD), "z", 0, 0, tiled=True)
    summed = jnp.sum(spread.astype(F32), axis=0).reshape(GROUP, -1, 4 * HD)
    final = lax.all_to_all(summed, "x", 0, 0, tiled=True)
    mixed_t, grad_tokens_t = call(
        head_sum_kernel, [((local, width), BF)] * 2, [place, mine, got]
    )
    share = final.shape[1]
    final = final.reshape(GROUP, share, 4, HD).transpose(1, 2, 0, 3).reshape(share, 4, local)
    return (mixed_t.T, grad_tokens_t.T, final[:, 1:], final[:, 0].T)


def solution(mesh):
    devices = mesh.devices.reshape(2, ROWS // 2, GROUP, 2, 2)
    fine = Mesh(devices, ("y", "z", "x", "h", "c"))
    placed = (
        P(SEQ_AXES, None),
        P(None, None, HEAD_AXES),
        P(HEAD_AXES, None),
        P(SEQ_AXES, None),
        P(SEQ_AXES, None),
        P(SEQ_AXES),
    )
    return jax.shard_map(
        on_device,
        mesh=fine,
        in_specs=placed,
        out_specs=(
            P(SEQ_AXES, HEAD_AXES),
            P(SEQ_AXES, HEAD_AXES),
            P(SEQ_AXES, None, HEAD_AXES),
            P(HEAD_AXES, SEQ_AXES),
        ),
        check_vma=False,
    )
```

profile of v0, /device:TPU:16, one launch (start us, length us, event | category | flops | bytes accessed | tf_op | source)
XLA Modules:
  0.0 152.1 jit_solution(10618896284044722112)
XLA Ops:
  7.3 6.7 %shard_map.93 = (bf16[336,384]{1,0:T(8,128)(2,1)}, bf16[336,384]{1,0:T(8,128)(2,1)}, bf16[336,384]{1,0:T(8,128)(2,1)}, bf16[336,384]{1,0:T(8,128)(2,1)}, bf16[2,192,1280]{2,1,0:T(8,128)(2,1)}) custom-call(s32[5]{0:T(128)S(1)} %stack.23.place, bf16[960,1280]{1,0:T(8,128)(2,1)} %bitcast.20, bf16[384,1280]{1,0:T(8,128)(2,1)} %tokens.1, ...), custom_call_target="tpu_custom_call" | custom-call | flops 1258291200 | bytes 8000000 | tf_op jit(solution)/shard_map/pallas_call | solution.py:55
  14.0 1.6 %collective-permute-start = (bf16[336,384]{1,0:T(8,128)(2,1)}, bf16[336,384]{1,0:T(8,128)(2,1)S(1)}, u32[]{:S(2)}, u32[]{:S(2)}) collective-permute-start(bf16[336,384]{1,0:T(8,128)(2,1)} %get-tuple-element.56), channel_id=1, source_target_pairs={{0,4},{4,8},{8,12},{12,0},{1,5},{5,9},{9,13},{13,1},{2,6},{6,10},{... | collective-permute-start | bytes 774152 | tf_op jit(solution)/shard_map/ppermute | solution.py:37
  15.6 2.7 %collective-permute-start.1 = (bf16[336,384]{1,0:T(8,128)(2,1)}, bf16[336,384]{1,0:T(8,128)(2,1)S(1)}, u32[]{:S(2)}, u32[]{:S(2)}) collective-permute-start(bf16[336,384]{1,0:T(8,128)(2,1)} %get-tuple-element.57), channel_id=1, source_target_pairs={{0,8},{4,12},{8,0},{12,4},{1,9},{5,13},{9,1},{13,5},{2,10},{6,14},... | collective-permute-start | bytes 774152 | tf_op jit(solution)/shard_map/ppermute | solution.py:37
  18.3 1.4 collective-permute-start.2
  19.8 3.9 %collective-permute-done.r1 = bf16[336,384]{1,0:T(8,128)(2,1)S(1)} collective-permute-done((bf16[336,384]{1,0:T(8,128)(2,1)}, bf16[336,384]{1,0:T(8,128)(2,1)S(1)}, u32[]{:S(2)}, u32[]{:S(2)}) %collective-permute-start) | collective-permute-done | bytes 258080 | tf_op jit(solution)/shard_map/ppermute | solution.py:37
  23.6 6.4 %collective-permute-done.1.r2 = bf16[336,384]{1,0:T(8,128)(2,1)S(1)} collective-permute-done((bf16[336,384]{1,0:T(8,128)(2,1)}, bf16[336,384]{1,0:T(8,128)(2,1)S(1)}, u32[]{:S(2)}, u32[]{:S(2)}) %collective-permute-start.1) | collective-permute-done | bytes 258080 | tf_op jit(solution)/shard_map/ppermute | solution.py:37
  31.7 6.6 %collective-permute-start.4 = (bf16[176,1152]{1,0:T(8,128)(2,1)S(1)}, bf16[176,1152]{1,0:T(8,128)(2,1)S(1)}, u32[]{:S(2)}, u32[]{:S(2)}) collective-permute-start(bf16[176,1152]{1,0:T(8,128)(2,1)S(1)} %get-tuple-element.60), channel_id=1, source_target_pairs={{0,240},{16,0},{32,16},{48,32},{64,48},{80,64},{96,80},{112,96},{1... | collective-permute-start | bytes 1216520 | tf_op jit(solution)/shard_map/ppermute | solution.py:37
  39.2 2.1 %shard_map.95 = (bf16[1280,960]{1,0:T(8,128)(2,1)S(1)}, bf16[1280,320]{1,0:T(8,128)(2,1)S(1)}, f32[4,16,3840]{2,1,0:T(8,128)S(1)}, bf16[4,384,80]{2,1,0:T(8,128)(2,1)S(1)}, f32[4,384,80]{2,1,0:T(8,128)S(1)}) custom-call(s32[5]{0:T(128)S(1)} %stack.23.place, bf16[336,384]{1,0:T(8,128)(2,1)S(1)} %copy-done.5, bf16[336,384]{1,0:T(8,128)(2,1)S(1)} %collective-permute-done.r1, ...), custom_call_target="tpu_custom_call" | custom-call | bytes 8000000 | tf_op jit(solution)/shard_map/pallas_call | solution.py:55
  41.4 1.6 %copy-done.2 = bf16[1280,960]{1,0:T(8,128)(2,1)} copy-done((bf16[1280,960]{1,0:T(8,128)(2,1)}, bf16[1280,960]{1,0:T(8,128)(2,1)S(1)}, u32[]{:S(2)}) %copy-start.2) | copy-done | bytes 2457624
  43.9 2.2 %collective-permute-done.4.from_next = bf16[176,1152]{1,0:T(8,128)(2,1)S(1)} collective-permute-done((bf16[176,1152]{1,0:T(8,128)(2,1)S(1)}, bf16[176,1152]{1,0:T(8,128)(2,1)S(1)}, u32[]{:S(2)}, u32[]{:S(2)}) %collective-permute-start.4) | collective-permute-done | bytes 405536 | tf_op jit(solution)/shard_map/ppermute | solution.py:37
  46.1 4.3 %collective-permute-done.3.from_prev = bf16[176,1152]{1,0:T(8,128)(2,1)S(1)} collective-permute-done((bf16[176,1152]{1,0:T(8,128)(2,1)S(1)}, bf16[176,1152]{1,0:T(8,128)(2,1)S(1)}, u32[]{:S(2)}, u32[]{:S(2)}) %collective-permute-start.3) | collective-permute-done | bytes 405536 | tf_op jit(solution)/shard_map/ppermute | solution.py:37
  50.4 19.1 %shard_map.96 = (bf16[160,1536]{1,0:T(8,128)(2,1)S(1)}, bf16[160,1152]{1,0:T(8,128)(2,1)S(1)}, bf16[160,1152]{1,0:T(8,128)(2,1)S(1)}, f32[160,1536]{1,0:T(8,128)...) custom-call(s32[5]{0:T(128)S(1)} %stack.23.place, ...), custom_call_target="tpu_custom_call" | custom-call | flops 6341787648 | bytes 6000000 | tf_op jit(solution)/shard_map/pallas_call | solution.py:55
  70.1 1.7 %collective-permute-start.9 = (bf16[160,1152]{1,0:T(8,128)(2,1)S(1)}, bf16[160,1152]{1,0:T(8,128)(2,1)S(1)}, u32[]{:S(2)}, u32[]{:S(2)}) collective-permute-start(bf16[160,1152]{1,0:T(8,128)(2,1)S(1)} %get-tuple-element.75), channel_id=1, source_target_pairs={{0,16},{16,32},{32,48},{48,64},{64,80},{80,96},{96,112},{112,128},... | collective-permute-start | bytes 1105928 | tf_op jit(solution)/shard_map/ppermute | solution.py:37
  71.8 4.8 %shard_map.97 = (f32[160,1280]{1,0:T(8,128)S(1)}, bf16[1536,1280]{1,0:T(8,128)(2,1)S(1)}) custom-call(s32[5]{0:T(128)S(1)} %stack.23.place, bf16[160,1536]{1,0:T(8,128)(2,1)S(1)} %get-tuple-element.76.values, bf16[8,2,192,1280]{3,2,1,0:T(8,128)(2,1)} %bitcast.22), custom_call_target="tpu_custom_call" | custom-call | tf_op jit(solution)/shard_map/pallas_call | solution.py:55
  76.6 1.5 collective-permute-done.8.from_next
  78.0 2.4 %collective-permute-done.9.from_prev = bf16[160,1152]{1,0:T(8,128)(2,1)S(1)} collective-permute-done((bf16[160,1152]{1,0:T(8,128)(2,1)S(1)}, bf16[160,1152]{1,0:T(8,128)(2,1)S(1)}, u32[]{:S(2)}, u32[]{:S(2)}) %collective-permute-start.9) | collective-permute-done | bytes 368672 | tf_op jit(solution)/shard_map/ppermute | solution.py:37
  81.3 2.0 %collective-permute-start.10 = (bf16[160,384]{1,0:T(8,128)(2,1)S(1)}, bf16[160,384]{1,0:T(8,128)(2,1)S(1)}, u32[]{:S(2)}, u32[]{:S(2)}) collective-permute-start(bf16[160,384]{1,0:T(8,128)(2,1)S(1)} %get-tuple-element.87), channel_id=1, source_target_pairs={{0,4},{4,8},{8,12},{12,0},{1,5},{5,9},{9,13},{13,1},{2,6},{6,10},{... | collective-permute-start | bytes 368648 | tf_op jit(solution)/shard_map/ppermute | solution.py:37
  83.2 3.8 %collective-permute-start.11 = (bf16[160,384]{1,0:T(8,128)(2,1)S(1)}, bf16[160,384]{1,0:T(8,128)(2,1)S(1)}, u32[]{:S(2)}, u32[]{:S(2)}) collective-permute-start(bf16[160,384]{1,0:T(8,128)(2,1)S(1)} %get-tuple-element.88), channel_id=1, source_target_pairs={{0,8},{4,12},{8,0},{12,4},{1,9},{5,13},{9,1},{13,5},{2,10},{6,14},... | collective-permute-start | bytes 368648 | tf_op jit(solution)/shard_map/ppermute | solution.py:37
  87.1 2.0 %collective-permute-start.5 = (bf16[160,384]{1,0:T(8,128)(2,1)S(1)}, bf16[160,384]{1,0:T(8,128)(2,1)S(1)}, u32[]{:S(2)}, u32[]{:S(2)}) collective-permute-start(bf16[160,384]{1,0:T(8,128)(2,1)S(1)} %get-tuple-element.71), channel_id=1, source_target_pairs={{0,4},{4,8},{8,12},{12,0},{1,5},{5,9},{9,13},{13,1},{2,6},{6,10},{... | collective-permute-start | bytes 368648 | tf_op jit(solution)/shard_map/ppermute | solution.py:37
  89.1 2.0 %collective-permute-done.10.refs_5_ = bf16[160,384]{1,0:T(8,128)(2,1)S(1)} collective-permute-done((bf16[160,384]{1,0:T(8,128)(2,1)S(1)}, bf16[160,384]{1,0:T(8,128)(2,1)S(1)}, u32[]{:S(2)}, u32[]{:S(2)}) %collective-permute-start.10) | collective-permute-done | bytes 122912 | tf_op jit(solution)/shard_map/ppermute | solution.py:37
  91.9 1.5 %shard_map.99 = (bf16[320,640]{1,0:T(8,128)(2,1)S(1)}, f32[320,640]{1,0:T(8,128)S(1)}) custom-call(s32[5]{0:T(128)S(1)} %stack.23.place, f32[160,1280]{1,0:T(8,128)S(1)} %get-tuple-element.79.early, bf16[160,1536]{1,0:T(8,128)(2,1)S(1)} %get-tuple-element.83.values, bf16[1536,1280]{1,0:T(8,128)(2,1)S(1)} %get-tuple-element.84.tokens), custom_call_target="tpu_custom_call" | custom-call | tf_op jit(solution)/shard_map/pallas_call | solution.py:55
  93.5 1.2 collective-permute-done.5.refs_1_
  94.7 1.3 collective-permute-done.6.refs_2_
  96.2 2.7 %shard_map.100 = (bf16[2,2,320,384]{3,2,1,0:T(8,128)(2,1)S(1)}, f32[2,2,320,384]{3,2,1,0:T(8,128)S(1)}) custom-call(s32[5]{0:T(128)S(1)} %stack.23.place, bf16[160,384]{1,0:T(8,128)(2,1)S(1)} %get-tuple-element.70.refs_0_, bf16[160,384]{1,0:T(8,128)(2,1)S(1)} %collective-permute-done.5.refs_1_, bf16[160,384]{1,0:T(8,128)(2,1)S(1)} %collective-permute-done.6.refs_2_, ...), custom_call_target="tpu_custom_call" | custom-call | tf_op jit(solution)/shard_map/pallas_call | solution.py:55
  100.0 1.6 %collective-permute-done.13.got = bf16[2,2,320,384]{3,2,1,0:T(8,128)(2,1)S(1)} collective-permute-done((bf16[2,2,320,384]{3,2,1,0:T(8,128)(2,1)S(1)}, bf16[2,2,320,384]{3,2,1,0:T(8,128)(2,1)S(1)}, u32[]{:S(2)}, u32[]{:S(2)}) %collective-permute-start.13) | collective-permute-done | bytes 983072 | tf_op jit(solution)/shard_map/ppermute | solution.py:37
  102.3 8.6 %collective-permute-done.14.got = bf16[320,640]{1,0:T(8,128)(2,1)S(1)} collective-permute-done((bf16[320,640]{1,0:T(8,128)(2,1)S(1)}, bf16[320,640]{1,0:T(8,128)(2,1)S(1)}, u32[]{:S(2)}, u32[]{:S(2)}) %collective-permute-start.14) | collective-permute-done | bytes 409632 | tf_op jit(solution)/shard_map/ppermute | solution.py:37
  111.0 1.5 %shard_map.103 = bf16[640,320]{1,0:T(8,128)(2,1)} custom-call(s32[5]{0:T(128)S(1)} %stack.23.place, f32[320,640]{1,0:T(8,128)S(1)} %get-tuple-element.104.keep, bf16[320,640]{1,0:T(8,128)(2,1)S(1)} %collective-permute-done.14.got), custom_call_target="tpu_custom_call" | custom-call | tf_op jit(solution)/shard_map/pallas_call | solution.py:55
  112.5 3.5 %all-to-all-start = ((bf16[8,80,320]{2,1,0:T(8,128)(2,1)}), bf16[8,80,320]{2,1,0:T(8,128)(2,1)S(1)}, u32[]{:S(2)}, u32[]{:S(2)}) async-start(bf16[8,80,320]{2,1,0:T(8,128)(2,1)} %bitcast.11), calls=%async_computation | async-start | bytes 983040 | tf_op jit(solution)/shard_map/all_to_all | solution.py:422
  116.9 15.9 %all-to-all-done = bf16[8,80,320]{2,1,0:T(8,128)(2,1)S(1)} async-done(((bf16[8,80,320]{2,1,0:T(8,128)(2,1)}), bf16[8,80,320]{2,1,0:T(8,128)(2,1)S(1)}, u32[]{:S(2)}, u32[]{:S(2)}) %all-to-all-start) | async-done | bytes 409632 | tf_op jit(solution)/shard_map/all_to_all | solution.py:422
  133.5 3.9 %all-to-all-start.1 = ((f32[4,20,320]{2,1,0:T(8,128)}), f32[4,20,320]{2,1,0:T(8,128)S(1)}, u32[]{:S(2)}, u32[]{:S(2)}) async-start(f32[4,20,320]{2,1,0:T(8,128)} %reshape.25), calls=%async_computation.1 | async-start | bytes 294912 | tf_op jit(solution)/shard_map/all_to_all | solution.py:424
  137.5 1.4 shard_map.102
  138.8 4.7 %all-to-all-done.1 = f32[4,20,320]{2,1,0:T(8,128)S(1)} async-done(((f32[4,20,320]{2,1,0:T(8,128)}), f32[4,20,320]{2,1,0:T(8,128)S(1)}, u32[]{:S(2)}, u32[]{:S(2)}) %all-to-all-start.1) | async-done | bytes 102432 | tf_op jit(solution)/shard_map/all_to_all | solution.py:424
  (47 shorter events, 11.2 us)
Async XLA Ops:
  7.2 64.6 %all-gather.3.cloned.1.call-start = ((), (), s32[]{:S(2)}) async-start(), calls=%async_computation.2 | async-start | bytes 8847360 | tf_op jit(solution)/shard_map/all_gather | solution.py:373
  7.3 31.0 %copy-start = (bf16[1280,3,320]{0,2,1:T(8,128)(2,1)S(1)}, bf16[1280,3,320]{0,2,1:T(8,128)(2,1)}, u32[]{:S(2)}) copy-start(bf16[1280,3,320]{0,2,1:T(8,128)(2,1)} %param.7) | copy-start | bytes 7372804
  7.3 31.0 %copy-start.1 = (bf16[320,1280]{1,0:T(8,128)(2,1)S(1)}, bf16[320,1280]{1,0:T(8,128)(2,1)}, u32[]{:S(2)}) copy-start(bf16[320,1280]{1,0:T(8,128)(2,1)} %w_out.3) | copy-start | bytes 2457604
  14.0 9.6 %collective-permute-start = (bf16[336,384]{1,0:T(8,128)(2,1)}, bf16[336,384]{1,0:T(8,128)(2,1)S(1)}, u32[]{:S(2)}, u32[]{:S(2)}) collective-permute-start(bf16[336,384]{1,0:T(8,128)(2,1)} %get-tuple-element.56), channel_id=1, source_target_pairs={{0,4},{4,8},{8,12},{12,0},{1,5},{5,9},{9,13},{13,1},{2,6},{6,10},{... | collective-permute-start | bytes 774152 | tf_op jit(solution)/shard_map/ppermute | solution.py:37
  15.6 14.4 %collective-permute-start.1 = (bf16[336,384]{1,0:T(8,128)(2,1)}, bf16[336,384]{1,0:T(8,128)(2,1)S(1)}, u32[]{:S(2)}, u32[]{:S(2)}) collective-permute-start(bf16[336,384]{1,0:T(8,128)(2,1)} %get-tuple-element.57), channel_id=1, source_target_pairs={{0,8},{4,12},{8,0},{12,4},{1,9},{5,13},{9,1},{13,5},{2,10},{6,14},... | collective-permute-start | bytes 774152 | tf_op jit(solution)/shard_map/ppermute | solution.py:37
  18.3 11.7 %collective-permute-start.2 = (bf16[336,384]{1,0:T(8,128)(2,1)}, bf16[336,384]{1,0:T(8,128)(2,1)S(1)}, u32[]{:S(2)}, u32[]{:S(2)}) collective-permute-start(bf16[336,384]{1,0:T(8,128)(2,1)} %get-tuple-element.58), channel_id=1, source_target_pairs={{0,12},{4,0},{8,4},{12,8},{1,13},{5,1},{9,5},{13,9},{2,14},{6,2},{... | collective-permute-start | bytes 774152 | tf_op jit(solution)/shard_map/ppermute | solution.py:37
  30.0 1.0 copy-start.4
  31.0 19.4 %copy-start.6 = (bf16[336,384]{1,0:T(8,128)(2,1)S(1)}, bf16[336,384]{1,0:T(8,128)(2,1)}, u32[]{:S(2)}) copy-start(bf16[336,384]{1,0:T(8,128)(2,1)} %get-tuple-element.55.r0) | copy-start | bytes 774148
  31.7 14.4 %collective-permute-start.4 = (bf16[176,1152]{1,0:T(8,128)(2,1)S(1)}, bf16[176,1152]{1,0:T(8,128)(2,1)S(1)}, u32[]{:S(2)}, u32[]{:S(2)}) collective-permute-start(bf16[176,1152]{1,0:T(8,128)(2,1)S(1)} %get-tuple-element.60), channel_id=1, source_target_pairs={{0,240},{16,0},{32,16},{48,32},{64,48},{80,64},{96,80},{112,96},{1... | collective-permute-start | bytes 1216520 | tf_op jit(solution)/shard_map/ppermute | solution.py:37
  38.3 12.1 %collective-permute-start.3 = (bf16[176,1152]{1,0:T(8,128)(2,1)S(1)}, bf16[176,1152]{1,0:T(8,128)(2,1)S(1)}, u32[]{:S(2)}, u32[]{:S(2)}) collective-permute-start(bf16[176,1152]{1,0:T(8,128)(2,1)S(1)} %get-tuple-element.59), channel_id=1, source_target_pairs={{0,16},{16,32},{32,48},{48,64},{64,80},{80,96},{96,112},{112,128},... | collective-permute-start | bytes 1216520 | tf_op jit(solution)/shard_map/ppermute | solution.py:37
  38.3 0.9 copy-start.5
  41.4 1.6 %copy-start.2 = (bf16[1280,960]{1,0:T(8,128)(2,1)}, bf16[1280,960]{1,0:T(8,128)(2,1)S(1)}, u32[]{:S(2)}) copy-start(bf16[1280,960]{1,0:T(8,128)(2,1)S(1)} %get-tuple-element.95.refs_9_) | copy-start | bytes 7372804
  42.9 1.0 copy-start.7
  69.5 8.5 %collective-permute-start.8 = (bf16[160,1152]{1,0:T(8,128)(2,1)S(1)}, bf16[160,1152]{1,0:T(8,128)(2,1)S(1)}, u32[]{:S(2)}, u32[]{:S(2)}) collective-permute-start(bf16[160,1152]{1,0:T(8,128)(2,1)S(1)} %get-tuple-element.74), channel_id=1, source_target_pairs={{0,240},{16,0},{32,16},{48,32},{64,48},{80,64},{96,80},{112,96},{1... | collective-permute-start | bytes 1105928 | tf_op jit(solution)/shard_map/ppermute | solution.py:37
  70.1 10.4 %collective-permute-start.9 = (bf16[160,1152]{1,0:T(8,128)(2,1)S(1)}, bf16[160,1152]{1,0:T(8,128)(2,1)S(1)}, u32[]{:S(2)}, u32[]{:S(2)}) collective-permute-start(bf16[160,1152]{1,0:T(8,128)(2,1)S(1)} %get-tuple-element.75), channel_id=1, source_target_pairs={{0,16},{16,32},{32,48},{48,64},{64,80},{80,96},{96,112},{112,128},... | collective-permute-start | bytes 1105928 | tf_op jit(solution)/shard_map/ppermute | solution.py:37
  81.3 9.8 %collective-permute-start.10 = (bf16[160,384]{1,0:T(8,128)(2,1)S(1)}, bf16[160,384]{1,0:T(8,128)(2,1)S(1)}, u32[]{:S(2)}, u32[]{:S(2)}) collective-permute-start(bf16[160,384]{1,0:T(8,128)(2,1)S(1)} %get-tuple-element.87), channel_id=1, source_target_pairs={{0,4},{4,8},{8,12},{12,0},{1,5},{5,9},{9,13},{13,1},{2,6},{6,10},{... | collective-permute-start | bytes 368648 | tf_op jit(solution)/shard_map/ppermute | solution.py:37
  83.2 10.3 %collective-permute-start.11 = (bf16[160,384]{1,0:T(8,128)(2,1)S(1)}, bf16[160,384]{1,0:T(8,128)(2,1)S(1)}, u32[]{:S(2)}, u32[]{:S(2)}) collective-permute-start(bf16[160,384]{1,0:T(8,128)(2,1)S(1)} %get-tuple-element.88), channel_id=1, source_target_pairs={{0,8},{4,12},{8,0},{12,4},{1,9},{5,13},{9,1},{13,5},{2,10},{6,14},... | collective-permute-start | bytes 368648 | tf_op jit(solution)/shard_map/ppermute | solution.py:37
  87.1 6.5 %collective-permute-start.12 = (bf16[160,384]{1,0:T(8,128)(2,1)S(1)}, bf16[160,384]{1,0:T(8,128)(2,1)S(1)}, u32[]{:S(2)}, u32[]{:S(2)}) collective-permute-start(bf16[160,384]{1,0:T(8,128)(2,1)S(1)} %get-tuple-element.89), channel_id=1, source_target_pairs={{0,12},{4,0},{8,4},{12,8},{1,13},{5,1},{9,5},{13,9},{2,14},{6,2},{... | collective-permute-start | bytes 368648 | tf_op jit(solution)/shard_map/ppermute | solution.py:37
  87.1 7.7 %collective-permute-start.5 = (bf16[160,384]{1,0:T(8,128)(2,1)S(1)}, bf16[160,384]{1,0:T(8,128)(2,1)S(1)}, u32[]{:S(2)}, u32[]{:S(2)}) collective-permute-start(bf16[160,384]{1,0:T(8,128)(2,1)S(1)} %get-tuple-element.71), channel_id=1, source_target_pairs={{0,4},{4,8},{8,12},{12,0},{1,5},{5,9},{9,13},{13,1},{2,6},{6,10},{... | collective-permute-start | bytes 368648 | tf_op jit(solution)/shard_map/ppermute | solution.py:37
  89.1 7.0 %collective-permute-start.6 = (bf16[160,384]{1,0:T(8,128)(2,1)S(1)}, bf16[160,384]{1,0:T(8,128)(2,1)S(1)}, u32[]{:S(2)}, u32[]{:S(2)}) collective-permute-start(bf16[160,384]{1,0:T(8,128)(2,1)S(1)} %get-tuple-element.72), channel_id=1, source_target_pairs={{0,8},{4,12},{8,0},{12,4},{1,9},{5,13},{9,1},{13,5},{2,10},{6,14},... | collective-permute-start | bytes 368648 | tf_op jit(solution)/shard_map/ppermute | solution.py:37
  91.1 5.1 %collective-permute-start.7 = (bf16[160,384]{1,0:T(8,128)(2,1)S(1)}, bf16[160,384]{1,0:T(8,128)(2,1)S(1)}, u32[]{:S(2)}, u32[]{:S(2)}) collective-permute-start(bf16[160,384]{1,0:T(8,128)(2,1)S(1)} %get-tuple-element.73), channel_id=1, source_target_pairs={{0,12},{4,0},{8,4},{12,8},{1,13},{5,1},{9,5},{13,9},{2,14},{6,2},{... | collective-permute-start | bytes 368648 | tf_op jit(solution)/shard_map/ppermute | solution.py:37
  91.9 4.4 %copy-start.3 = (bf16[1280,960]{1,0:T(8,128)(2,1)S(1)}, bf16[1280,960]{1,0:T(8,128)(2,1)}, u32[]{:S(2)}) copy-start(bf16[1280,960]{1,0:T(8,128)(2,1)} %copy-done.2) | copy-start | bytes 7372804
  91.9 4.4 %copy-start.8 = (bf16[1280,320]{1,0:T(8,128)(2,1)S(1)}, bf16[1280,320]{1,0:T(8,128)(2,1)}, u32[]{:S(2)}) copy-start(bf16[1280,320]{1,0:T(8,128)(2,1)} %copy-done.7) | copy-start | bytes 2457604
  99.0 2.7 %collective-permute-start.13 = (bf16[2,2,320,384]{3,2,1,0:T(8,128)(2,1)S(1)}, bf16[2,2,320,384]{3,2,1,0:T(8,128)(2,1)S(1)}, u32[]{:S(2)}, u32[]{:S(2)}) collective-permute-start(bf16[2,2,320,384]{3,2,1,0:T(8,128)(2,1)S(1)} %get-tuple-element.97), channel_id=1, source_target_pairs={{0,1},{1,0},{2,3},{3,2},{4,5},{5,4},{6,7},{7,6},{8,9},{9,8},{10,11... | collective-permute-start | bytes 2949128 | tf_op jit(solution)/shard_map/ppermute | solution.py:37
  99.1 11.9 %collective-permute-start.14 = (bf16[320,640]{1,0:T(8,128)(2,1)S(1)}, bf16[320,640]{1,0:T(8,128)(2,1)S(1)}, u32[]{:S(2)}, u32[]{:S(2)}) collective-permute-start(bf16[320,640]{1,0:T(8,128)(2,1)S(1)} %get-tuple-element.99), channel_id=1, source_target_pairs={{0,128},{128,0},{1,129},{129,1},{2,130},{130,2},{3,131},{131,3},{4... | collective-permute-start | bytes 1228808 | tf_op jit(solution)/shard_map/ppermute | solution.py:37
  112.5 20.3 %all-to-all-start = ((bf16[8,80,320]{2,1,0:T(8,128)(2,1)}), bf16[8,80,320]{2,1,0:T(8,128)(2,1)S(1)}, u32[]{:S(2)}, u32[]{:S(2)}) async-start(bf16[8,80,320]{2,1,0:T(8,128)(2,1)} %bitcast.11), calls=%async_computation | async-start | bytes 983040 | tf_op jit(solution)/shard_map/all_to_all | solution.py:422
  116.0 21.5 %collective-permute-start.15 = (bf16[2,320,384]{2,1,0:T(8,128)(2,1)S(1)}, bf16[2,320,384]{2,1,0:T(8,128)(2,1)S(1)}, u32[]{:S(2)}, u32[]{:S(2)}) collective-permute-start(bf16[2,320,384]{2,1,0:T(8,128)(2,1)S(1)} %get-tuple-element.101), channel_id=1, source_target_pairs={{0,2},{2,0},{1,3},{3,1},{4,6},{6,4},{5,7},{7,5},{8,10},{10,8},{9,1... | collective-permute-start | bytes 1474568 | tf_op jit(solution)/shard_map/ppermute | solution.py:37
  133.5 10.0 %all-to-all-start.1 = ((f32[4,20,320]{2,1,0:T(8,128)}), f32[4,20,320]{2,1,0:T(8,128)S(1)}, u32[]{:S(2)}, u32[]{:S(2)}) async-start(f32[4,20,320]{2,1,0:T(8,128)} %reshape.25), calls=%async_computation.1 | async-start | bytes 294912 | tf_op jit(solution)/shard_map/all_to_all | solution.py:424
Sparse Core Ops, SparseCore 0:
  14.1 52.8 all-gather.2
where the time goes:
time: 152 us
  waiting for transfers between devices  56.2 us (37%)
  Pallas kernels  42 us (28%)
  starting transfers between devices  32.6 us (21%)
  between operations  14.2 us (9%)
  local copies, waits for them, and re-layouts  6.98 us (5%)
    pallas_call x11, Pallas kernels, call(): pl.pallas_call(kernel, out_shape=[kept.get(c, jax.ShapeDtypeStruct)(s, d)...  42 us
    ppermute x16, waiting for transfers between devices, shift(): lax.ppermute(value, axis, [(i, (i + steps) % count) for i in range(count)])  35.7 us
    ppermute x16, starting transfers between devices, shift(): lax.ppermute(value, axis, [(i, (i + steps) % count) for i in range(count)])  25.2 us
    all_to_all x1, waiting for transfers between devices, on_device(): lax.all_to_all(half_w.reshape(ROWS // 2, model // ROWS, 4 * HD), 'z', 0,...  15.9 us
    unnamed x20, local copies, waits for them, and re-layouts  5.78 us
    all_to_all x1, waiting for transfers between devices, on_device(): final = lax.all_to_all(summed, 'x', 0, 0, tiled=True)  4.69 us
    all_to_all x1, starting transfers between devices, on_device(): final = lax.all_to_all(summed, 'x', 0, 0, tiled=True)  3.95 us
    all_to_all x1, starting transfers between devices, on_device(): lax.all_to_all(half_w.reshape(ROWS // 2, model // ROWS, 4 * HD), 'z', 0,...  3.48 us
  transfers between devices with their start and end apart: 19, of which 15 were waited for; matrix products, arithmetic and copies ran while one was open for 0% of the time, Pallas kernels for 20%

commit v1 on v0

v1 whole, which is shorter than its diff:
```python
import functools

import jax
import jax.numpy as jnp
from jax import lax
from jax.experimental import pallas as pl
from jax.experimental.pallas import tpu as pltpu
from jax.sharding import Mesh
from jax.sharding import PartitionSpec as P

HD = 80
BLOCK = 128
SPAN = 3
TOK = 384
GROUP = 4
PIECES = GROUP + 2 * SPAN
WINDOW = 2 * SPAN + 1
ROW = GROUP * TOK
HALO = SPAN * TOK
KEYS = PIECES * TOK
ROWS = 16
NB = 192
SCALE = HD ** (-0.5)
LOG2E = 1.4426950408889634
NEG = -1e30
BF = jnp.bfloat16
F32 = jnp.float32
MIB = 1024 * 1024
SENT = 4 * HD + 16
WIDE = ROW // 2
MAIN = 256
ROW_AXES = ("y", "z")
SEQ_AXES = ("y", "z", "x")
HEAD_AXES = ("h", "c")


def shift(value, axis, steps):
    count = lax.axis_size(axis)
    return lax.ppermute(value, axis, [(i, (i + steps) % count) for i in range(count)])


def spec_vmem():
    return pl.BlockSpec(memory_space=pltpu.VMEM)


def spec_smem():
    return pl.BlockSpec(memory_space=pltpu.SMEM)


def call(kernel, outs, ins, scratch=(), mib=12, flops=0, moved=0, exps=0, spaces=None, out_spaces=None):
    anywhere = pl.BlockSpec(memory_space=pl.ANY)
    spec = {"v": spec_vmem(), "s": spec_smem(), "a": anywhere, "h": anywhere, "f": spec_vmem()}
    kept = {"h": pltpu.HBM, "f": pltpu.VMEM}
    spaces = spaces or "s" + "v" * (len(ins) - 1)
    out_spaces = out_spaces or "v" * len(outs)
    ins = [pltpu.with_memory_space_constraint(a, kept[c]) if c in kept else a for a, c in zip(ins, spaces)]
    return pl.pallas_call(
        kernel,
        out_shape=[kept.get(c, jax.ShapeDtypeStruct)(s, d) for (s, d), c in zip(outs, out_spaces)],
        in_specs=[spec[c] for c in spaces],
        out_specs=[spec[c] for c in out_spaces],
        scratch_shapes=list(scratch),
        compiler_params=pltpu.CompilerParams(vmem_limit_bytes=mib * MIB),
        cost_estimate=pl.CostEstimate(flops=flops, bytes_accessed=moved, transcendentals=exps),
    )(*ins)


def dot_nn(a, b):
    return lax.dot_general(a, b, (((1,), (0,)), ((), ())), preferred_element_type=F32)


def dot_nt(a, b):
    return lax.dot_general(a, b, (((1,), (1,)), ((), ())), preferred_element_type=F32)


def project_kernel(place, w, tokens, w_out, cotangent, regions, mask, o0, o1, o2, o3, parts,
                   wv, tv, wov, cv, rv, mv, extra, held, stage, sems):
    x = place[1]
    half = tokens.shape[0] // 2
    mine = pl.ds(pl.multiple_of(place[3] * half, half), half)
    pairs = ((w, wv), (tokens, tv), (w_out, wov), (cotangent, cv), (regions, rv), (mask, mv))
    copies = [pltpu.make_async_copy(a, b, sems.at[n]) for n, (a, b) in enumerate(pairs)]
    for n in (1, 0, 3, 2, 4, 5):
        copies[n].start()
    copies[4].wait()
    copies[5].wait()
    extra[...] = jnp.zeros_like(extra)
    extra[0:1, :] = rv[...].reshape(1, -1).astype(F32)
    extra[1:4, :NB] = mv[...].astype(F32)
    copies[1].wait()
    copies[0].wait()
    width = tokens.shape[0]
    held[:3] = dot_nt(wv[...], tv[...]).astype(BF).reshape(3, GROUP, HD, width)
    copies[3].wait()
    copies[2].wait()
    held[3] = dot_nt(wov[...], cv[...]).astype(BF).reshape(GROUP, HD, width)
    outs = []
    for k, out in enumerate((o0, o1, o2, o3)):
        head = lax.rem(x + k, GROUP)
        into = out if k == 0 else stage.at[k]
        for piece in range(3):
            into[piece * HD : (piece + 1) * HD, :] = held[piece, head]
        into[3 * HD : 3 * HD + 16, :] = extra[...].astype(BF)
        into[3 * HD + 16 :, :] = held[3, head]
        if k > 0:
            outs.append(pltpu.make_async_copy(into, out, sems.at[6 + k]))
    outs.append(pltpu.make_async_copy(tv.at[mine], parts.at[0], sems.at[10]))
    outs.append(pltpu.make_async_copy(cv.at[mine], parts.at[1], sems.at[11]))
    for copy in outs:
        copy.start()
    for copy in outs:
        copy.wait()


def dot_tn(a, b):
    return lax.dot_general(a, b, (((0,), (0,)), ((), ())), preferred_element_type=F32)


def halo_kernel(place, r0, r1, r2, r3, to_next, to_prev):
    x = place[1]
    for k, ref in enumerate((r0, r1, r2, r3)):
        pos = lax.rem(x - k + GROUP, GROUP)

        @pl.when(pos >= 1)
        def _():
            at = pl.multiple_of((pos - 1) * TOK, TOK)
            to_next[:, pl.ds(at, TOK)] = ref[HD : 3 * HD + 16, :]

        @pl.when(pos <= 2)
        def _():
            at = pl.multiple_of(pos * TOK, TOK)
            to_prev[:, pl.ds(at, TOK)] = ref[HD : 3 * HD + 16, :]


def block_rows(i):
    return slice(i * BLOCK, (i + 1) * BLOCK)


def open_regions(eff, key_reg, first, i):
    opened = eff > 0.5
    if first is not None:
        blocks = lax.broadcasted_iota(jnp.int32, eff.shape, 1) // BLOCK
        opened = opened | (blocks == first + i)
    return jnp.where(opened, key_reg, -1.0)


def lane_sum(p):
    total = p[:, :BLOCK]
    for g in range(1, p.shape[1] // BLOCK):
        total = total + p[:, g * BLOCK : (g + 1) * BLOCK]
    return jnp.sum(total, axis=1, keepdims=True)


def lane_max(s):
    top = s[:, :BLOCK]
    for g in range(1, s.shape[1] // BLOCK):
        top = jnp.maximum(top, s[:, g * BLOCK : (g + 1) * BLOCK])
    return jnp.max(top, axis=1, keepdims=True)


def own_forward_kernel(place, r0, r1, r2, r3,
                       p1, m1, l1, o1, qn, don, qt, kt, vt, reg, eff_far,
                       eff_own, s_ref):
    row = place[0]
    x = place[1]
    lane = lax.broadcasted_iota(jnp.int32, (256, KEYS), 1) // BLOCK
    per_row = ROW // BLOCK
    per_halo = HALO // BLOCK
    ahead = jnp.where(lane < per_row, lane, jnp.where(lane < per_row + per_halo, lane - per_row - per_halo, lane - per_halo))
    block_id = lax.rem(ahead + row * per_row + NB, NB)
    pick = jnp.where(block_id == lax.broadcasted_iota(jnp.int32, (256, KEYS), 0), 1.0, 0.0).astype(BF)
    for k, ref in enumerate((r0, r1, r2, r3)):
        pos = lax.rem(x - k + GROUP, GROUP)
        cols = pl.ds(pl.multiple_of(pos * TOK, TOK), TOK)
        extra = ref[3 * HD : 3 * HD + 16, :]
        eff = dot_nn(extra[:, :256], pick)
        eff_own[pos] = eff[:, :ROW]
        eff_far[pos] = eff[:, ROW:]
        reg[:, cols] = extra.astype(F32)
        qt[:, cols] = ref[:HD, :]
        kt[:, cols] = ref[HD : 2 * HD, :]
        vt[:, cols] = ref[2 * HD : 3 * HD, :]
        qn[pos] = ref[:HD, :].astype(F32).T.astype(BF)
        don[pos] = ref[3 * HD + 16 :, :].astype(F32).T

    tops = []
    for r in range(GROUP):
        rows = slice(r * TOK, (r + 1) * TOK)
        reg_q = reg[:, rows].T[:, 0:1]
        raw = dot_nn(qn[r], kt[...])
        top = []
        for i in range(3):
            key_eff = open_regions(eff_own[r, 1 + i : 2 + i, :], reg[0:1, :], 3 * r, i)
            s = jnp.where(reg_q[block_rows(i)] == key_eff, raw[block_rows(i)], NEG)
            s_ref[r, block_rows(i), :] = s
            top.append(lane_max(s))
        tops.append(jnp.concatenate(top, axis=0))
        m1[r] = tops[r]
    for r in range(GROUP):
        rows = slice(r * TOK, (r + 1) * TOK)
        p = jnp.exp2((s_ref[r] - tops[r]) * (SCALE * LOG2E))
        p1[rows, :] = p.astype(BF)
        l1[r] = lane_sum(p)
        o1[r] = dot_nt(p1[rows, :], vt[...])


def far_kernel(place, eff_far, reg, qn, don, m1, l1, o1, qt, from_prev, from_next,
               gp, gn, attn, dos1, delta1, dq2,
               kh, vh, regh, s_ref, p_ref, ds_ref, dk, dv):
    for ref, cols in ((from_prev, slice(0, HALO)), (from_next, slice(HALO, 2 * HALO))):
        kh[:, cols] = ref[:HD, :]
        vh[:, cols] = ref[HD : 2 * HD, :]
        regh[:, cols] = ref[2 * HD :, :].astype(F32)
    dk[...] = jnp.zeros_like(dk)
    dv[...] = jnp.zeros_like(dv)

    tops = []
    for r in range(GROUP):
        rows = slice(r * TOK, (r + 1) * TOK)
        win = slice(r * TOK, r * TOK + HALO)
        reg_q = reg[:, rows].T[:, 0:1]
        raw = dot_nn(qn[r], kh[:, win])
        top = []
        for i in range(3):
            key_eff = open_regions(eff_far[r, 1 + i : 2 + i, win], regh[0:1, win], None, i)
            s = jnp.where(reg_q[block_rows(i)] == key_eff, raw[block_rows(i)], NEG)
            s_ref[r, block_rows(i), :] = s
            top.append(lane_max(s))
        tops.append(jnp.maximum(jnp.concatenate(top, axis=0), 0.1 * NEG))
    held = []
    for r in range(GROUP):
        win = slice(r * TOK, r * TOK + HALO)
        p = jnp.exp2((s_ref[r] - tops[r]) * (SCALE * LOG2E))
        p_ref[r] = p.astype(BF)
        held.append((lane_sum(p), dot_nt(p_ref[r], vh[:, win])))
    stats = []
    for r in range(GROUP):
        rows = slice(r * TOK, (r + 1) * TOK)
        m2 = tops[r]
        l2, o2 = held[r]
        m = jnp.maximum(m1[r], m2)
        w1 = jnp.exp2((m1[r] - m) * (SCALE * LOG2E))
        w2 = jnp.exp2((m2 - m) * (SCALE * LOG2E))
        inv = 1.0 / (l1[r] * w1 + l2 * w2)
        w1 = w1 * inv
        w2 = w2 * inv
        at_n = (o1[r] * w1 + o2 * w2).astype(BF).astype(F32)
        do_n = don[r]
        near = (do_n * (w1 * SCALE)).astype(BF)
        far = (do_n * (w2 * SCALE)).astype(BF)
        dos1[rows, :] = near
        delta1[r] = jnp.sum(near.astype(F32) * at_n, axis=1, keepdims=True)
        attn[:, rows] = at_n.T.astype(BF)
        stats.append((far, jnp.sum(far.astype(F32) * at_n, axis=1, keepdims=True)))
    for r in range(GROUP):
        rows = slice(r * TOK, (r + 1) * TOK)
        win = slice(r * TOK, r * TOK + HALO)
        far, delta2 = stats[r]
        dp = dot_nn(far, vh[:, win])
        ds_ref[r] = (p_ref[r].astype(F32) * (dp - delta2)).astype(BF)
        dq2[r] = dot_nt(ds_ref[r], kh[:, win])
    for r in range(GROUP):
        rows = slice(r * TOK, (r + 1) * TOK)
        win = slice(r * TOK, r * TOK + HALO)
        dk[:, win] += dot_nn(qt[:, rows], ds_ref[r])
        dv[:, win] += dot_nn(stats[r][0].astype(F32).T.astype(BF), p_ref[r])
    for out, cols in ((gp, slice(0, HALO)), (gn, slice(HALO, 2 * HALO))):
        out[:HD, :] = dk[:, cols].astype(BF)
        out[HD:, :] = (dv[:, cols] * (1.0 / SCALE)).astype(BF)


def own_backward_kernel(place, p1, dos1, delta1, dq2, qt, kt, vt, dq, own, ds_ref):
    def step(r, carry):
        rows = pl.ds(pl.multiple_of(r * TOK, TOK), TOK)
        d_q = dq2[r]
        near = dos1[rows, :]
        for c in range(2):
            cols = slice(c * WIDE, (c + 1) * WIDE)
            dp = dot_nn(near, vt[:, cols])
            ds = (p1[rows, cols].astype(F32) * (dp - delta1[r])).astype(BF)
            ds_ref[rows, cols] = ds
            d_q = d_q + dot_nt(ds, kt[:, cols])
        dq[:, rows] = d_q.T.astype(BF)
        return carry

    lax.fori_loop(0, GROUP, step, 0, unroll=True)
    dos_t = dos1[...].astype(F32).T.astype(BF)
    for c in range(2):
        cols = slice(c * WIDE, (c + 1) * WIDE)
        own[:HD, cols] = dot_nn(qt[...], ds_ref[:, cols])
        own[HD:, cols] = dot_nn(dos_t, p1[:, cols]) * (1.0 / SCALE)


def own_forward(place, parts):
    stat = ((GROUP, TOK, 1), F32)
    wide = ((GROUP, TOK, HD), F32)
    flat = ((HD, ROW), BF)
    outs = [((ROW, ROW), BF), stat, stat, wide, ((GROUP, TOK, HD), BF), wide, flat, flat, flat]
    outs = outs + [((16, ROW), F32), ((GROUP, 16, 2 * HALO), F32)]
    return call(
        own_forward_kernel, outs, [place, *parts],
        [pltpu.VMEM((GROUP, 16, ROW), F32), pltpu.VMEM((GROUP, TOK, ROW), F32)],
        mib=24, out_spaces="f" * len(outs),
        flops=4 * ROW * ROW * 128, moved=6_000_000, exps=ROW * ROW,
    )


def far_part(place, ins):
    outs = [((2 * HD, HALO), BF)] * 2 + [((HD, ROW), BF), ((ROW, HD), BF), ((GROUP, TOK, 1), F32)]
    outs = outs + [((GROUP, TOK, HD), F32)]
    scratch = [
        pltpu.VMEM((HD, 2 * HALO), BF),
        pltpu.VMEM((HD, 2 * HALO), BF),
        pltpu.VMEM((16, 2 * HALO), F32),
        pltpu.VMEM((GROUP, TOK, HALO), F32),
        pltpu.VMEM((GROUP, TOK, HALO), BF),
        pltpu.VMEM((GROUP, TOK, HALO), BF),
        pltpu.VMEM((HD, 2 * HALO), F32),
        pltpu.VMEM((HD, 2 * HALO), F32),
    ]
    return call(
        far_kernel, outs, [place, *ins], scratch, mib=28, out_spaces="f" * len(outs),
        flops=12 * ROW * HALO * 128, moved=6_000_000, exps=ROW * HALO,
    )


def own_backward(place, ins):
    return call(
        own_backward_kernel, [((HD, ROW), BF), ((2 * HD, ROW), F32)], [place, *ins],
        [pltpu.VMEM((ROW, ROW), BF)], mib=24, out_spaces="ff",
        flops=8 * ROW * ROW * 128, moved=6_000_000,
    )


def combine_kernel(place, attn, dq, own, from_next, from_prev, full, c0, c1, c2, c3):
    x = place[1]
    full[:HD, :] = attn[...]
    full[HD : 2 * HD, :] = dq[...]
    full[2 * HD :, :TOK] = (own[:, :TOK] + from_prev[:, :TOK].astype(F32)).astype(BF)
    middle = own[:, TOK:HALO] + from_next[:, : HALO - TOK].astype(F32)
    full[2 * HD :, TOK:HALO] = (middle + from_prev[:, TOK:].astype(F32)).astype(BF)
    full[2 * HD :, HALO:] = (own[:, HALO:] + from_next[:, HALO - TOK :].astype(F32)).astype(BF)
    for k, out in enumerate((c0, c1, c2, c3)):
        at = pl.multiple_of(lax.rem(x + k, GROUP) * TOK, TOK)
        out[...] = full[:, pl.ds(at, TOK)]


def weights_kernel(scale, place, values, gathered, out, tokens, cotangent, sems):
    parts, _, part_rows, _ = gathered.shape
    copies = []
    for which, into in ((0, tokens), (1, cotangent)):
        for n in range(parts):
            to = into.at[n * part_rows : (n + 1) * part_rows]
            copies.append(pltpu.make_async_copy(gathered.at[n, which], to, sems.at[which, n]))
    for copy in copies:
        copy.start()
    for copy in copies[:parts]:
        copy.wait()
    grads = dot_nn(values[HD:, :], tokens[...])
    for copy in copies[parts:]:
        copy.wait()
    total = (jnp.concatenate([dot_nn(values[:HD, :], cotangent[...]), grads], axis=0) * scale).T
    count = out.shape[0]
    rows = total.shape[0] // (2 * count)
    for z in range(count):
        first = total[z * rows : (z + 1) * rows]
        second = total[(count + z) * rows : (count + z + 1) * rows]
        both = jnp.concatenate([first, second], axis=0)
        out[z, : 2 * rows, :] = both[:, :MAIN].astype(BF)
        fold = rows // 2
        rest = [both[g * fold : (g + 1) * fold, MAIN:] for g in range(4)]
        folded = jnp.concatenate([jnp.concatenate(rest, axis=1), jnp.zeros((8, MAIN), F32)], axis=0)
        out[z, 2 * rows :, :] = folded.astype(BF)


def row_sum_kernel(place, spread, out):
    total = jnp.sum(spread[...].astype(F32), axis=0)
    count, share, _ = out.shape
    rest = count * share
    for n in range(count):
        at = rest + (n % 2) * share
        left = (n // 2) * (4 * HD - MAIN)
        out[n, :, :MAIN] = total[n * share : (n + 1) * share]
        out[n, :, MAIN:] = total[at : at + share, left : left + 4 * HD - MAIN]


def order_kernel(place, final, grad_qkv, grad_out):
    for h in range(GROUP):
        piece = final[h] + final[GROUP + h]
        cols = slice(h * HD, (h + 1) * HD)
        grad_out[:, cols] = piece[:, :HD]
        for part in range(3):
            grad_qkv[part, :, cols] = piece[:, (part + 1) * HD : (part + 2) * HD]


def share_kernel(place, *refs):
    ins, (w_out, w, send, keep, attn, grads, whole) = refs[:GROUP], refs[GROUP:]
    x = place[1]
    core = place[3]
    for k in range(GROUP):
        head = lax.rem(x - k + GROUP, GROUP)
        attn[head] = ins[k][:HD, :]
        for part in range(3):
            grads[part, head] = ins[k][(part + 1) * HD : (part + 2) * HD, :]
    local = GROUP * HD
    for n, (weights, held) in enumerate(((w_out, attn), (w, grads))):
        values = held[...].reshape(-1, TOK)
        whole[...] = dot_tn(weights[...], values)
        for other, out in ((1, send), (0, keep)):
            for h in range(2):
                at = pl.multiple_of((2 * h + lax.rem(core + other, 2)) * local, local)
                out[n, h] = whole[pl.ds(at, local), :].astype(out.dtype)


def core_sum_kernel(place, keep, got, other, mine):
    h = place[4]
    for n in range(2):
        other[n] = (keep[n, 1 - h] + got[n, 1 - h].astype(F32)).astype(BF)
        mine[n] = keep[n, h] + got[n, h].astype(F32)


def head_sum_kernel(place, mine, got, mixed, grad):
    mixed[...] = (mine[0] + got[0].astype(F32)).astype(BF)
    grad[...] = (mine[1] + got[1].astype(F32)).astype(BF)


def scatter_core(place, values, w_out, w):
    local, model = w_out.shape
    shape = (2, 2, local, TOK)
    send, keep = call(
        share_kernel,
        [(shape, BF), (shape, F32)],
        [place, *values, w_out, w],
        [
            pltpu.VMEM((GROUP, HD, TOK), BF),
            pltpu.VMEM((3, GROUP, HD, TOK), BF),
            pltpu.VMEM((model, TOK), F32),
        ],
        mib=16, out_spaces="ff",
    )
    got = shift(send, "c", 1)
    return call(
        core_sum_kernel, [((2, local, TOK), BF), ((2, local, TOK), F32)], [place, keep, got],
        out_spaces="ff",
    )


def on_device(tokens, w_qkv, w_out, cotangent, block_mask, regions):
    width, model = tokens.shape
    local = w_out.shape[0]
    x = lax.axis_index("x")
    y = lax.axis_index("y")
    row = y * (ROWS // 2) + lax.axis_index("z")
    place = jnp.stack([row, x, y, lax.axis_index("c"), lax.axis_index("h")]).astype(jnp.int32)
    grad_scale = (width * lax.axis_size(SEQ_AXES)) ** (-0.5)
    w2 = w_qkv.transpose(1, 2, 0).reshape(3 * local, model)

    *sent, parts_mine = call(
        project_kernel,
        [((SENT, width), BF)] * GROUP + [((2, width // 2, model), BF)],
        [place, w2, tokens, w_out, cotangent, regions, block_mask],
        [
            pltpu.VMEM((3 * local, model), BF),
            pltpu.VMEM((width, model), BF),
            pltpu.VMEM((local, model), BF),
            pltpu.VMEM((width, model), BF),
            pltpu.VMEM(regions.shape, jnp.int32),
            pltpu.VMEM(block_mask.shape, jnp.int32),
            pltpu.VMEM((16, width), F32),
            pltpu.VMEM((4, GROUP, HD, width), BF),
            pltpu.VMEM((GROUP, SENT, width), BF),
            pltpu.SemaphoreType.DMA((12,)),
        ],
        mib=16, spaces="shhhhhh", out_spaces="fhhhh",
        flops=2 * 4 * local * model * width, moved=8_000_000,
    )
    parts = [sent[0]] + [shift(sent[k], "x", k) for k in (1, 2, 3)]
    gathered = lax.all_gather(parts_mine, ("x", "c"), axis=0)
    to_next, to_prev = call(
        halo_kernel, [((2 * HD + 16, HALO), BF)] * 2, [place, *parts], moved=2_000_000
    )
    from_prev = shift(to_next, ROW_AXES, 1)
    from_next = shift(to_prev, ROW_AXES, -1)
    held = own_forward(place, parts)
    p1, m1, l1, o1, qn, don, qt, kt, vt, reg, eff_far = held

    gp, gn, attn, dos1, delta1, dq2 = far_part(
        place, [eff_far, reg, qn, don, m1, l1, o1, qt, from_prev, from_next]
    )
    back_next = shift(gp, ROW_AXES, -1)
    back_prev = shift(gn, ROW_AXES, 1)
    dq, own = own_backward(place, [p1, dos1, delta1, dq2, qt, kt, vt])
    d_all, *chunks = call(
        combine_kernel, [((4 * HD, ROW), BF)] + [((4 * HD, width), BF)] * GROUP,
        [place, attn, dq, own, back_next, back_prev], out_spaces="f" * 5,
    )
    kv_all = [chunks[0]] + [shift(chunks[k], "x", k) for k in (1, 2, 3)]
    share = model // ROWS // GROUP
    gathered, d_all = lax.optimization_barrier((gathered, d_all))
    (terms,) = call(
        functools.partial(weights_kernel, grad_scale),
        [((ROWS // 2, 8 * share + 48, MAIN), BF)],
        [place, d_all, gathered],
        [
            pltpu.VMEM((ROW, model), BF),
            pltpu.VMEM((ROW, model), BF),
            pltpu.SemaphoreType.DMA((2, 2 * GROUP)),
        ],
        spaces="svh", out_spaces="f", mib=20,
    )
    spread = lax.all_to_all(terms, "z", 0, 0, tiled=True)
    other, mine = scatter_core(place, kv_all, w_out, w2)
    got = shift(other, "h", 1)
    (summed,) = call(row_sum_kernel, [((2 * GROUP, share, 4 * HD), F32)], [place, spread], out_spaces="f")
    final = lax.all_to_all(summed, ("y", "x"), 0, 0, tiled=True)
    mixed_t, grad_tokens_t = call(head_sum_kernel, [((local, width), BF)] * 2, [place, mine, got])
    final, mixed_t = lax.optimization_barrier((final, mixed_t))
    grad_qkv_t, grad_out_t = call(
        order_kernel, [((3, share, local), F32), ((share, local), F32)], [place, final]
    )
    return (mixed_t.T, grad_tokens_t.T, grad_qkv_t.transpose(1, 0, 2), grad_out_t.T)


def solution(mesh):
    devices = mesh.devices.reshape(2, ROWS // 2, GROUP, 2, 2)
    fine = Mesh(devices, ("y", "z", "x", "h", "c"))
    placed = (
        P(SEQ_AXES, None),
        P(None, None, HEAD_AXES),
        P(HEAD_AXES, None),
        P(SEQ_AXES, None),
        P(SEQ_AXES, None),
        P(SEQ_AXES),
    )
    return jax.shard_map(
        on_device,
        mesh=fine,
        in_specs=placed,
        out_specs=(
            P(SEQ_AXES, HEAD_AXES),
            P(SEQ_AXES, HEAD_AXES),
            P(SEQ_AXES, None, HEAD_AXES),
            P(HEAD_AXES, SEQ_AXES),
        ),
        check_vma=False,
    )
```

time: 152 us -> 129 us (0.85)
  waiting for transfers between devices: 56.2 us -> 37.9 us
  local copies, waits for them, and re-layouts: 6.98 us -> 2.87 us
  starting transfers between devices: 32.6 us -> 30.7 us
    ppermute x16 -> x12, waiting for transfers between devices: 35.7 us -> 20.7 us  [shift(): lax.ppermute(value, axis, [(i, (i + steps) % count) for i in range(count)])]
    all_to_all x2, waiting for transfers between devices: 20.6 us -> 17.1 us  [the longest x1 11.1 us: on_device(): spread = lax.all_to_all(terms, 'z', 0, 0, tiled=True)]
    unnamed x20 -> x8, local copies, waits for them, and re-layouts: 5.78 us -> 2.78 us
    ppermute x16 -> x12, starting transfers between devices: 25.2 us -> 23.7 us  [shift(): lax.ppermute(value, axis, [(i, (i + steps) % count) for i in range(count)])]
    pallas_call x11 -> x12, Pallas kernels: 42 us -> 43.5 us  [call(): pl.pallas_call(kernel, out_shape=[kept.get(c, jax.ShapeDtypeStruct)(s, d)...]
  transfers between devices with their start and end apart: 19 -> 15, of which waited for: 15 -> 8; matrix products, arithmetic and copies ran while one was open for 0% -> 0% of each run, Pallas kernels for 20% -> 28%
where the time goes in v1:
time: 129 us
  Pallas kernels  43.5 us (34%)
  waiting for transfers between devices  37.9 us (29%)
  starting transfers between devices  30.7 us (24%)
  between operations  14.2 us (11%)
  local copies, waits for them, and re-layouts  2.87 us (2%)
    pallas_call x12, Pallas kernels, call(): pl.pallas_call(kernel, out_shape=[kept.get(c, jax.ShapeDtypeStruct)(s, d)...  43.5 us
    ppermute x12, starting transfers between devices, shift(): lax.ppermute(value, axis, [(i, (i + steps) % count) for i in range(count)])  23.7 us
    ppermute x12, waiting for transfers between devices, shift(): lax.ppermute(value, axis, [(i, (i + steps) % count) for i in range(count)])  20.7 us
    all_to_all x1, waiting for transfers between devices, on_device(): spread = lax.all_to_all(terms, 'z', 0, 0, tiled=True)  11.1 us
    all_to_all x1, waiting for transfers between devices, on_device(): final = lax.all_to_all(summed, ('y', 'x'), 0, 0, tiled=True)  6.01 us
    all_to_all x1, starting transfers between devices, on_device(): spread = lax.all_to_all(terms, 'z', 0, 0, tiled=True)  3.56 us
    all_to_all x1, starting transfers between devices, on_device(): final = lax.all_to_all(summed, ('y', 'x'), 0, 0, tiled=True)  3.42 us
    unnamed x8, local copies, waits for them, and re-layouts  2.78 us
  transfers between devices with their start and end apart: 15, of which 8 were waited for; matrix products, arithmetic and copies ran while one was open for 0% of the time, Pallas kernels for 28%

profile of v1, /device:TPU:16, one launch (start us, length us, event | category | flops | bytes accessed | tf_op | source)
XLA Modules:
  0.0 129.1 jit_solution(8880352491003970727)
XLA Ops:
  7.3 6.6 %shard_map.93 = (bf16[336,384]{1,0:T(8,128)(2,1)S(1)}, bf16[336,384]{1,0:T(8,128)(2,1)}, bf16[336,384]{1,0:T(8,128)(2,1)}, bf16[336,384]{1,0:T(8,128)(2,1)}, bf16[2,192,1280]{2,1,0:T(8,128)(2,1)}) custom-call(s32[5]{0:T(128)S(1)} %stack.23.place, bf16[960,1280]{1,0:T(8,128)(2,1)} %bitcast.13, bf16[384,1280]{1,0:T(8,128)(2,1)} %tokens.1, ...), custom_call_target="tpu_custom_call" | custom-call | flops 1258291200 | bytes 8000000 | tf_op jit(solution)/shard_map/pallas_call | solution.py:57
  13.9 1.6 %collective-permute-start = (bf16[336,384]{1,0:T(8,128)(2,1)}, bf16[336,384]{1,0:T(8,128)(2,1)S(1)}, u32[]{:S(2)}, u32[]{:S(2)}) collective-permute-start(bf16[336,384]{1,0:T(8,128)(2,1)} %get-tuple-element.49), channel_id=1, source_target_pairs={{0,4},{4,8},{8,12},{12,0},{1,5},{5,9},{9,13},{13,1},{2,6},{6,10},{... | collective-permute-start | bytes 774152 | tf_op jit(solution)/shard_map/ppermute | solution.py:39
  15.5 2.7 %collective-permute-start.1 = (bf16[336,384]{1,0:T(8,128)(2,1)}, bf16[336,384]{1,0:T(8,128)(2,1)S(1)}, u32[]{:S(2)}, u32[]{:S(2)}) collective-permute-start(bf16[336,384]{1,0:T(8,128)(2,1)} %get-tuple-element.50), channel_id=1, source_target_pairs={{0,8},{4,12},{8,0},{12,4},{1,9},{5,13},{9,1},{13,5},{2,10},{6,14},... | collective-permute-start | bytes 774152 | tf_op jit(solution)/shard_map/ppermute | solution.py:39
  18.3 1.4 %collective-permute-start.2 = (bf16[336,384]{1,0:T(8,128)(2,1)}, bf16[336,384]{1,0:T(8,128)(2,1)S(1)}, u32[]{:S(2)}, u32[]{:S(2)}) collective-permute-start(bf16[336,384]{1,0:T(8,128)(2,1)} %get-tuple-element.51), channel_id=1, source_target_pairs={{0,12},{4,0},{8,4},{12,8},{1,13},{5,1},{9,5},{13,9},{2,14},{6,2},{... | collective-permute-start | bytes 774152 | tf_op jit(solution)/shard_map/ppermute | solution.py:39
  19.7 3.9 %collective-permute-done.r1 = bf16[336,384]{1,0:T(8,128)(2,1)S(1)} collective-permute-done((bf16[336,384]{1,0:T(8,128)(2,1)}, bf16[336,384]{1,0:T(8,128)(2,1)S(1)}, u32[]{:S(2)}, u32[]{:S(2)}) %collective-permute-start) | collective-permute-done | bytes 258080 | tf_op jit(solution)/shard_map/ppermute | solution.py:39
  23.5 6.4 %collective-permute-done.1.r2 = bf16[336,384]{1,0:T(8,128)(2,1)S(1)} collective-permute-done((bf16[336,384]{1,0:T(8,128)(2,1)}, bf16[336,384]{1,0:T(8,128)(2,1)S(1)}, u32[]{:S(2)}, u32[]{:S(2)}) %collective-permute-start.1) | collective-permute-done | bytes 258080 | tf_op jit(solution)/shard_map/ppermute | solution.py:39
  30.6 2.0 %collective-permute-start.3 = (bf16[176,1152]{1,0:T(8,128)(2,1)S(1)}, bf16[176,1152]{1,0:T(8,128)(2,1)S(1)}, u32[]{:S(2)}, u32[]{:S(2)}) collective-permute-start(bf16[176,1152]{1,0:T(8,128)(2,1)S(1)} %get-tuple-element.60), channel_id=1, source_target_pairs={{0,16},{16,32},{32,48},{48,64},{64,80},{80,96},{96,112},{112,128},... | collective-permute-start | bytes 1216520 | tf_op jit(solution)/shard_map/ppermute | solution.py:39
  32.6 4.9 %collective-permute-start.4 = (bf16[176,1152]{1,0:T(8,128)(2,1)S(1)}, bf16[176,1152]{1,0:T(8,128)(2,1)S(1)}, u32[]{:S(2)}, u32[]{:S(2)}) collective-permute-start(bf16[176,1152]{1,0:T(8,128)(2,1)S(1)} %get-tuple-element.61), channel_id=1, source_target_pairs={{0,240},{16,0},{32,16},{48,32},{64,48},{80,64},{96,80},{112,96},{1... | collective-permute-start | bytes 1216520 | tf_op jit(solution)/shard_map/ppermute | solution.py:39
  37.5 5.9 %shard_map.94 = (bf16[1536,1536]{1,0:T(8,128)(2,1)S(1)}, f32[4,384,1]{2,1,0:T(8,128)S(1)}, f32[4,384,1]{2,1,0:T(8,128)S(1)}, f32[4,384,80]{2,1,0:T(8,128)S(1)}, ...) custom-call(s32[5]{0:T(128)S(1)} %stack.23.place, ...), custom_call_target="tpu_custom_call" | custom-call | flops 1207959552 | bytes 6000000 | tf_op jit(solution)/shard_map/pallas_call | solution.py:57
  43.4 2.4 %collective-permute-done.3.from_prev = bf16[176,1152]{1,0:T(8,128)(2,1)S(1)} collective-permute-done((bf16[176,1152]{1,0:T(8,128)(2,1)S(1)}, bf16[176,1152]{1,0:T(8,128)(2,1)S(1)}, u32[]{:S(2)}, u32[]{:S(2)}) %collective-permute-start.3) | collective-permute-done | bytes 405536 | tf_op jit(solution)/shard_map/ppermute | solution.py:39
  45.8 7.9 %shard_map.96 = (bf16[160,1152]{1,0:T(8,128)(2,1)S(1)}, bf16[160,1152]{1,0:T(8,128)(2,1)S(1)}, bf16[80,1536]{1,0:T(8,128)(2,1)S(1)}, bf16[1536,80]{1,0:T(8,128)(...) custom-call(s32[5]{0:T(128)S(1)} %stack.23.place, f32[4,16,2304]{2,1,0:T(8,128)S(1)} %get-tuple-element.52.eff_far, ...), custom_call_target="tpu_custom_call" | custom-call | flops 2717908992 | bytes 6000000 | tf_op jit(solution)/shard_map/pallas_call | solution.py:57
  53.7 4.4 %collective-permute-start.5 = (bf16[160,1152]{1,0:T(8,128)(2,1)S(1)}, bf16[160,1152]{1,0:T(8,128)(2,1)S(1)}, u32[]{:S(2)}, u32[]{:S(2)}) collective-permute-start(bf16[160,1152]{1,0:T(8,128)(2,1)S(1)} %get-tuple-element.71), channel_id=1, source_target_pairs={{0,240},{16,0},{32,16},{48,32},{64,48},{80,64},{96,80},{112,96},{1... | collective-permute-start | bytes 1105928 | tf_op jit(solution)/shard_map/ppermute | solution.py:39
  58.1 4.8 %shard_map.97 = (bf16[80,1536]{1,0:T(8,128)(2,1)S(1)}, f32[160,1536]{1,0:T(8,128)S(1)}) custom-call(s32[5]{0:T(128)S(1)} %stack.23.place, bf16[1536,1536]{1,0:T(8,128)(2,1)S(1)} %get-tuple-element.63.p1, bf16[1536,80]{1,0:T(8,128)(2,1)S(1)} %get-tuple-element.64.dos1, f32[4,384,1]{2,1,0:T(8,128)S(1)} %get-tuple-element.65.delta1, ...), custom_call_target="tpu_custom_call" | custom-call | flops 2415919104 | bytes 6000000 | tf_op jit(solution)/shard_map/pallas_call | solution.py:57
  63.0 1.2 collective-permute-done.5.from_next
  64.2 4.3 %collective-permute-done.6.from_prev = bf16[160,1152]{1,0:T(8,128)(2,1)S(1)} collective-permute-done((bf16[160,1152]{1,0:T(8,128)(2,1)S(1)}, bf16[160,1152]{1,0:T(8,128)(2,1)S(1)}, u32[]{:S(2)}, u32[]{:S(2)}) %collective-permute-start.6) | collective-permute-done | bytes 368672 | tf_op jit(solution)/shard_map/ppermute | solution.py:39
  68.5 1.7 %shard_map.98 = (bf16[320,1536]{1,0:T(8,128)(2,1)S(1)}, bf16[320,384]{1,0:T(8,128)(2,1)S(1)}, bf16[320,384]{1,0:T(8,128)(2,1)}, bf16[320,384]{1,0:T(8,128)(2,1)}, bf16[320,384]{1,0:T(8,128)(2,1)}) custom-call(s32[5]{0:T(128)S(1)} %stack.23.place, bf16[80,1536]{1,0:T(8,128)(2,1)S(1)} %get-tuple-element.62.attn, bf16[80,1536]{1,0:T(8,128)(2,1)S(1)} %get-tuple-element.69.dq, ...), custom_call_target="tpu_custom_call" | custom-call | tf_op jit(solution)/shard_map/pallas_call | solution.py:57
  70.1 0.7 copy-done.2
  70.8 2.0 %collective-permute-start.7 = (bf16[320,384]{1,0:T(8,128)(2,1)}, bf16[320,384]{1,0:T(8,128)(2,1)}, u32[]{:S(2)}, u32[]{:S(2)}) collective-permute-start(bf16[320,384]{1,0:T(8,128)(2,1)} %get-tuple-element.77), channel_id=1, source_target_pairs={{0,4},{4,8},{8,12},{12,0},{1,5},{5,9},{9,13},{13,1},{2,6},{6,10},{... | collective-permute-start | bytes 737288 | tf_op jit(solution)/shard_map/ppermute | solution.py:39
  72.8 3.9 %collective-permute-start.8 = (bf16[320,384]{1,0:T(8,128)(2,1)}, bf16[320,384]{1,0:T(8,128)(2,1)}, u32[]{:S(2)}, u32[]{:S(2)}) collective-permute-start(bf16[320,384]{1,0:T(8,128)(2,1)} %get-tuple-element.78), channel_id=1, source_target_pairs={{0,8},{4,12},{8,0},{12,4},{1,9},{5,13},{9,1},{13,5},{2,10},{6,14},... | collective-permute-start | bytes 737288 | tf_op jit(solution)/shard_map/ppermute | solution.py:39
  76.7 6.1 %shard_map.99 = bf16[8,208,256]{2,1,0:T(8,128)(2,1)} custom-call(s32[5]{0:T(128)S(1)} %stack.23.place, bf16[320,1536]{1,0:T(8,128)(2,1)S(1)} %get-tuple-element.74.values, bf16[8,2,192,1280]{3,2,1,0:T(8,128)(2,1)} %bitcast.15), custom_call_target="tpu_custom_call" | custom-call | tf_op jit(solution)/shard_map/pallas_call | solution.py:57
  82.8 3.6 %all-to-all-start = ((bf16[8,208,256]{2,1,0:T(8,128)(2,1)}), bf16[8,208,256]{2,1,0:T(8,128)(2,1)S(1)}, u32[]{:S(2)}, u32[]{:S(2)}) async-start(bf16[8,208,256]{2,1,0:T(8,128)(2,1)} %shard_map.99), calls=%async_computation | async-start | bytes 1703936 | tf_op jit(solution)/shard_map/all_to_all | solution.py:511
  86.5 1.1 copy-done.1
  87.6 0.9 copy-done.3
  88.5 4.1 %shard_map.101 = (bf16[2,2,320,384]{3,2,1,0:T(8,128)(2,1)S(1)}, f32[2,2,320,384]{3,2,1,0:T(8,128)S(1)}) custom-call(s32[5]{0:T(128)S(1)} %stack.23.place, bf16[320,384]{1,0:T(8,128)(2,1)S(1)} %copy-done.3, bf16[320,384]{1,0:T(8,128)(2,1)} %collective-permute-done.7.refs_1_, bf16[320,384]{1,0:T(8,128)(2,1)} %collective-permute-done.8.refs_2_, ...), custom_call_target="tpu_custom_call" | custom-call | tf_op jit(solution)/shard_map/pallas_call | solution.py:57
  92.8 2.6 %collective-permute-done.10.got = bf16[2,2,320,384]{3,2,1,0:T(8,128)(2,1)S(1)} collective-permute-done((bf16[2,2,320,384]{3,2,1,0:T(8,128)(2,1)S(1)}, bf16[2,2,320,384]{3,2,1,0:T(8,128)(2,1)S(1)}, u32[]{:S(2)}, u32[]{:S(2)}) %collective-permute-start.10) | collective-permute-done | bytes 983072 | tf_op jit(solution)/shard_map/ppermute | solution.py:39
  95.3 1.5 %shard_map.102 = (bf16[2,320,384]{2,1,0:T(8,128)(2,1)}, f32[2,320,384]{2,1,0:T(8,128)S(1)}) custom-call(s32[5]{0:T(128)S(1)} %stack.23.place, f32[2,2,320,384]{3,2,1,0:T(8,128)S(1)} %get-tuple-element.80.keep, bf16[2,2,320,384]{3,2,1,0:T(8,128)(2,1)S(1)} %collective-permute-done.10.got), custom_call_target="tpu_custom_call" | custom-call | tf_op jit(solution)/shard_map/pallas_call | solution.py:57
  97.5 11.1 %all-to-all-done.spread = bf16[8,208,256]{2,1,0:T(8,128)(2,1)S(1)} async-done(((bf16[8,208,256]{2,1,0:T(8,128)(2,1)}), bf16[8,208,256]{2,1,0:T(8,128)(2,1)S(1)}, u32[]{:S(2)}, u32[]{:S(2)}) %all-to-all-start) | async-done | bytes 852000 | tf_op jit(solution)/shard_map/all_to_all | solution.py:511
  108.7 1.4 %shard_map.100 = f32[8,20,320]{2,1,0:T(8,128)} custom-call(s32[5]{0:T(128)S(1)} %stack.23.place, bf16[8,208,256]{2,1,0:T(8,128)(2,1)S(1)} %all-to-all-done.spread), custom_call_target="tpu_custom_call" | custom-call | tf_op jit(solution)/shard_map/pallas_call | solution.py:57
  110.1 3.4 %all-to-all-start.1 = ((f32[8,20,320]{2,1,0:T(8,128)}), f32[8,20,320]{2,1,0:T(8,128)S(1)}, u32[]{:S(2)}, u32[]{:S(2)}) async-start(f32[8,20,320]{2,1,0:T(8,128)} %shard_map.100), calls=%async_computation.1 | async-start | bytes 589824 | tf_op jit(solution)/shard_map/all_to_all | solution.py:515
  113.5 1.4 %shard_map.103 = (bf16[320,384]{1,0:T(8,128)(2,1)}, bf16[320,384]{1,0:T(8,128)(2,1)}) custom-call(s32[5]{0:T(128)S(1)} %stack.23.place, f32[2,320,384]{2,1,0:T(8,128)S(1)} %get-tuple-element.82.mine, bf16[2,320,384]{2,1,0:T(8,128)(2,1)S(1)} %collective-permute-done.11.got), custom_call_target="tpu_custom_call" | custom-call | tf_op jit(solution)/shard_map/pallas_call | solution.py:57
  114.9 6.0 %all-to-all-done.1.final = f32[8,20,320]{2,1,0:T(8,128)S(1)} async-done(((f32[8,20,320]{2,1,0:T(8,128)}), f32[8,20,320]{2,1,0:T(8,128)S(1)}, u32[]{:S(2)}, u32[]{:S(2)}) %all-to-all-start.1) | async-done | bytes 204832 | tf_op jit(solution)/shard_map/all_to_all | solution.py:515
  120.9 1.3 %shard_map.104 = (f32[3,20,320]{2,1,0:T(8,128)}, f32[20,320]{1,0:T(8,128)}) custom-call(s32[5]{0:T(128)S(1)} %stack.23.place, f32[8,20,320]{2,1,0:T(8,128)S(1)} %all-to-all-done.1.final), custom_call_target="tpu_custom_call" | custom-call | tf_op jit(solution)/shard_map/pallas_call | solution.py:57
  (20 shorter events, 1.6 us)
Async XLA Ops:
  7.2 69.5 %all-gather.3.cloned.1.call-start = ((), (), s32[]{:S(2)}) async-start(), calls=%async_computation.2 | async-start | bytes 8847360 | tf_op jit(solution)/shard_map/all_gather | solution.py:478
  13.9 9.6 %collective-permute-start = (bf16[336,384]{1,0:T(8,128)(2,1)}, bf16[336,384]{1,0:T(8,128)(2,1)S(1)}, u32[]{:S(2)}, u32[]{:S(2)}) collective-permute-start(bf16[336,384]{1,0:T(8,128)(2,1)} %get-tuple-element.49), channel_id=1, source_target_pairs={{0,4},{4,8},{8,12},{12,0},{1,5},{5,9},{9,13},{13,1},{2,6},{6,10},{... | collective-permute-start | bytes 774152 | tf_op jit(solution)/shard_map/ppermute | solution.py:39
  15.5 14.4 %collective-permute-start.1 = (bf16[336,384]{1,0:T(8,128)(2,1)}, bf16[336,384]{1,0:T(8,128)(2,1)S(1)}, u32[]{:S(2)}, u32[]{:S(2)}) collective-permute-start(bf16[336,384]{1,0:T(8,128)(2,1)} %get-tuple-element.50), channel_id=1, source_target_pairs={{0,8},{4,12},{8,0},{12,4},{1,9},{5,13},{9,1},{13,5},{2,10},{6,14},... | collective-permute-start | bytes 774152 | tf_op jit(solution)/shard_map/ppermute | solution.py:39
  18.3 11.7 %collective-permute-start.2 = (bf16[336,384]{1,0:T(8,128)(2,1)}, bf16[336,384]{1,0:T(8,128)(2,1)S(1)}, u32[]{:S(2)}, u32[]{:S(2)}) collective-permute-start(bf16[336,384]{1,0:T(8,128)(2,1)} %get-tuple-element.51), channel_id=1, source_target_pairs={{0,12},{4,0},{8,4},{12,8},{1,13},{5,1},{9,5},{13,9},{2,14},{6,2},{... | collective-permute-start | bytes 774152 | tf_op jit(solution)/shard_map/ppermute | solution.py:39
  30.6 15.2 %collective-permute-start.3 = (bf16[176,1152]{1,0:T(8,128)(2,1)S(1)}, bf16[176,1152]{1,0:T(8,128)(2,1)S(1)}, u32[]{:S(2)}, u32[]{:S(2)}) collective-permute-start(bf16[176,1152]{1,0:T(8,128)(2,1)S(1)} %get-tuple-element.60), channel_id=1, source_target_pairs={{0,16},{16,32},{32,48},{48,64},{64,80},{80,96},{96,112},{112,128},... | collective-permute-start | bytes 1216520 | tf_op jit(solution)/shard_map/ppermute | solution.py:39
  32.6 13.2 %collective-permute-start.4 = (bf16[176,1152]{1,0:T(8,128)(2,1)S(1)}, bf16[176,1152]{1,0:T(8,128)(2,1)S(1)}, u32[]{:S(2)}, u32[]{:S(2)}) collective-permute-start(bf16[176,1152]{1,0:T(8,128)(2,1)S(1)} %get-tuple-element.61), channel_id=1, source_target_pairs={{0,240},{16,0},{32,16},{48,32},{64,48},{80,64},{96,80},{112,96},{1... | collective-permute-start | bytes 1216520 | tf_op jit(solution)/shard_map/ppermute | solution.py:39
  53.7 10.5 %collective-permute-start.5 = (bf16[160,1152]{1,0:T(8,128)(2,1)S(1)}, bf16[160,1152]{1,0:T(8,128)(2,1)S(1)}, u32[]{:S(2)}, u32[]{:S(2)}) collective-permute-start(bf16[160,1152]{1,0:T(8,128)(2,1)S(1)} %get-tuple-element.71), channel_id=1, source_target_pairs={{0,240},{16,0},{32,16},{48,32},{64,48},{80,64},{96,80},{112,96},{1... | collective-permute-start | bytes 1105928 | tf_op jit(solution)/shard_map/ppermute | solution.py:39
  58.1 10.4 %collective-permute-start.6 = (bf16[160,1152]{1,0:T(8,128)(2,1)S(1)}, bf16[160,1152]{1,0:T(8,128)(2,1)S(1)}, u32[]{:S(2)}, u32[]{:S(2)}) collective-permute-start(bf16[160,1152]{1,0:T(8,128)(2,1)S(1)} %get-tuple-element.72), channel_id=1, source_target_pairs={{0,16},{16,32},{32,48},{48,64},{64,80},{80,96},{96,112},{112,128},... | collective-permute-start | bytes 1105928 | tf_op jit(solution)/shard_map/ppermute | solution.py:39
  70.1 0.7 copy-start.2
  70.8 15.6 %collective-permute-start.7 = (bf16[320,384]{1,0:T(8,128)(2,1)}, bf16[320,384]{1,0:T(8,128)(2,1)}, u32[]{:S(2)}, u32[]{:S(2)}) collective-permute-start(bf16[320,384]{1,0:T(8,128)(2,1)} %get-tuple-element.77), channel_id=1, source_target_pairs={{0,4},{4,8},{8,12},{12,0},{1,5},{5,9},{9,13},{13,1},{2,6},{6,10},{... | collective-permute-start | bytes 737288 | tf_op jit(solution)/shard_map/ppermute | solution.py:39
  72.8 13.6 %collective-permute-start.8 = (bf16[320,384]{1,0:T(8,128)(2,1)}, bf16[320,384]{1,0:T(8,128)(2,1)}, u32[]{:S(2)}, u32[]{:S(2)}) collective-permute-start(bf16[320,384]{1,0:T(8,128)(2,1)} %get-tuple-element.78), channel_id=1, source_target_pairs={{0,8},{4,12},{8,0},{12,4},{1,9},{5,13},{9,1},{13,5},{2,10},{6,14},... | collective-permute-start | bytes 737288 | tf_op jit(solution)/shard_map/ppermute | solution.py:39
  76.7 9.7 %collective-permute-start.9 = (bf16[320,384]{1,0:T(8,128)(2,1)}, bf16[320,384]{1,0:T(8,128)(2,1)}, u32[]{:S(2)}, u32[]{:S(2)}) collective-permute-start(bf16[320,384]{1,0:T(8,128)(2,1)} %get-tuple-element.79), channel_id=1, source_target_pairs={{0,12},{4,0},{8,4},{12,8},{1,13},{5,1},{9,5},{13,9},{2,14},{6,2},{... | collective-permute-start | bytes 737288 | tf_op jit(solution)/shard_map/ppermute | solution.py:39
  76.7 9.7 %copy-start = (bf16[1280,3,320]{0,2,1:T(8,128)(2,1)S(1)}, bf16[1280,3,320]{0,2,1:T(8,128)(2,1)}, u32[]{:S(2)}) copy-start(bf16[1280,3,320]{0,2,1:T(8,128)(2,1)} %param.7) | copy-start | bytes 7372804
  82.8 25.8 %all-to-all-start = ((bf16[8,208,256]{2,1,0:T(8,128)(2,1)}), bf16[8,208,256]{2,1,0:T(8,128)(2,1)S(1)}, u32[]{:S(2)}, u32[]{:S(2)}) async-start(bf16[8,208,256]{2,1,0:T(8,128)(2,1)} %shard_map.99), calls=%async_computation | async-start | bytes 1703936 | tf_op jit(solution)/shard_map/all_to_all | solution.py:511
  86.4 1.1 copy-start.1
  87.6 0.9 copy-start.3
  92.7 2.7 %collective-permute-start.10 = (bf16[2,2,320,384]{3,2,1,0:T(8,128)(2,1)S(1)}, bf16[2,2,320,384]{3,2,1,0:T(8,128)(2,1)S(1)}, u32[]{:S(2)}, u32[]{:S(2)}) collective-permute-start(bf16[2,2,320,384]{3,2,1,0:T(8,128)(2,1)S(1)} %get-tuple-element.81), channel_id=1, source_target_pairs={{0,1},{1,0},{2,3},{3,2},{4,5},{5,4},{6,7},{7,6},{8,9},{9,8},{10,11... | collective-permute-start | bytes 2949128 | tf_op jit(solution)/shard_map/ppermute | solution.py:39
  96.8 16.7 %collective-permute-start.11 = (bf16[2,320,384]{2,1,0:T(8,128)(2,1)}, bf16[2,320,384]{2,1,0:T(8,128)(2,1)S(1)}, u32[]{:S(2)}, u32[]{:S(2)}) collective-permute-start(bf16[2,320,384]{2,1,0:T(8,128)(2,1)} %get-tuple-element.83), channel_id=1, source_target_pairs={{0,2},{2,0},{1,3},{3,1},{4,6},{6,4},{5,7},{7,5},{8,10},{10,8},{9,1... | collective-permute-start | bytes 1474568 | tf_op jit(solution)/shard_map/ppermute | solution.py:39
  110.1 10.8 %all-to-all-start.1 = ((f32[8,20,320]{2,1,0:T(8,128)}), f32[8,20,320]{2,1,0:T(8,128)S(1)}, u32[]{:S(2)}, u32[]{:S(2)}) async-start(f32[8,20,320]{2,1,0:T(8,128)} %shard_map.100), calls=%async_computation.1 | async-start | bytes 589824 | tf_op jit(solution)/shard_map/all_to_all | solution.py:515
Sparse Core Ops, SparseCore 0:
  14.1 52.8 all-gather.2

commit v2 on v1

--- a/solution.py
+++ b/solution.py
@@ -26,7 +26,7 @@
 BF = jnp.bfloat16
 F32 = jnp.float32
 MIB = 1024 * 1024
-SENT = 4 * HD + 16
+SENT = 3 * HD + 16
 WIDE = ROW // 2
 MAIN = 256
 ROW_AXES = ("y", "z")
@@ -73,43 +73,58 @@
     return lax.dot_general(a, b, (((1,), (1,)), ((), ())), preferred_element_type=F32)
 
 
-def project_kernel(place, w, tokens, w_out, cotangent, regions, mask, o0, o1, o2, o3, parts,
-                   wv, tv, wov, cv, rv, mv, extra, held, stage, sems):
-    x = place[1]
+def halves_kernel(place, tokens, cotangent, parts, held, sems):
     half = tokens.shape[0] // 2
     mine = pl.ds(pl.multiple_of(place[3] * half, half), half)
-    pairs = ((w, wv), (tokens, tv), (w_out, wov), (cotangent, cv), (regions, rv), (mask, mv))
+    loads = [pltpu.make_async_copy(a.at[mine], held.at[n], sems.at[n]) for n, a in enumerate((tokens, cotangent))]
+    stores = [pltpu.make_async_copy(held.at[n], parts.at[n], sems.at[2 + n]) for n in range(2)]
+    for copy in loads:
+        copy.start()
+    for load, store in zip(loads, stores):
+        load.wait()
+        store.start()
+    for copy in stores:
+        copy.wait()
+
+
+def project_kernel(place, w, tokens, regions, mask, o0, o1, o2, o3, wv, tv, rv, mv, extra, held, stage, sems):
+    x = place[1]
+    width = tokens.shape[0]
+    local = GROUP * HD
+    pairs = [(tokens, tv)] + [(w.at[n * local : (n + 1) * local], wv.at[n]) for n in range(3)]
+    pairs = pairs + [(regions, rv), (mask, mv)]
     copies = [pltpu.make_async_copy(a, b, sems.at[n]) for n, (a, b) in enumerate(pairs)]
-    for n in (1, 0, 3, 2, 4, 5):
-        copies[n].start()
+    for copy in copies:
+        copy.start()
+    outs = []
+    copies[0].wait()
+    for n in range(3):
+        copies[1 + n].wait()
+        held[n] = dot_nt(wv[n], tv[...]).astype(BF).reshape(GROUP, HD, width)
     copies[4].wait()
     copies[5].wait()
     extra[...] = jnp.zeros_like(extra)
     extra[0:1, :] = rv[...].reshape(1, -1).astype(F32)
     extra[1:4, :NB] = mv[...].astype(F32)
-    copies[1].wait()
-    copies[0].wait()
-    width = tokens.shape[0]
-    held[:3] = dot_nt(wv[...], tv[...]).astype(BF).reshape(3, GROUP, HD, width)
-    copies[3].wait()
-    copies[2].wait()
-    held[3] = dot_nt(wov[...], cv[...]).astype(BF).reshape(GROUP, HD, width)
-    outs = []
     for k, out in enumerate((o0, o1, o2, o3)):
         head = lax.rem(x + k, GROUP)
         into = out if k == 0 else stage.at[k]
         for piece in range(3):
             into[piece * HD : (piece + 1) * HD, :] = held[piece, head]
-        into[3 * HD : 3 * HD + 16, :] = extra[...].astype(BF)
-        into[3 * HD + 16 :, :] = held[3, head]
+        into[3 * HD :, :] = extra[...].astype(BF)
         if k > 0:
-            outs.append(pltpu.make_async_copy(into, out, sems.at[6 + k]))
-    outs.append(pltpu.make_async_copy(tv.at[mine], parts.at[0], sems.at[10]))
-    outs.append(pltpu.make_async_copy(cv.at[mine], parts.at[1], sems.at[11]))
-    for copy in outs:
-        copy.start()
+            copy = pltpu.make_async_copy(into, out, sems.at[8 + k])
+            copy.start()
+            outs.append(copy)
     for copy in outs:
         copy.wait()
+
+
+def project_grad_kernel(place, w_out, cotangent, o0, o1, o2, o3, held):
+    x = place[1]
+    held[...] = dot_nt(w_out[...], cotangent[...]).astype(BF).reshape(GROUP, HD, -1)
+    for k, out in enumerate((o0, o1, o2, o3)):
+        out[...] = held[lax.rem(x + k, GROUP)]
 
 
 def dot_tn(a, b):
@@ -159,7 +174,7 @@
 
 
 def own_forward_kernel(place, r0, r1, r2, r3,
-                       p1, m1, l1, o1, qn, don, qt, kt, vt, reg, eff_far,
+                       p1, m1, l1, o1, qn, qt, kt, vt, reg, eff_far,
                        eff_own, s_ref):
     row = place[0]
     x = place[1]
@@ -181,7 +196,6 @@
         kt[:, cols] = ref[HD : 2 * HD, :]
         vt[:, cols] = ref[2 * HD : 3 * HD, :]
         qn[pos] = ref[:HD, :].astype(F32).T.astype(BF)
-        don[pos] = ref[3 * HD + 16 :, :].astype(F32).T
 
     tops = []
     for r in range(GROUP):
@@ -204,9 +218,12 @@
         o1[r] = dot_nt(p1[rows, :], vt[...])
 
 
-def far_kernel(place, eff_far, reg, qn, don, m1, l1, o1, qt, from_prev, from_next,
+def far_kernel(place, d0, d1, d2, d3, eff_far, reg, qn, m1, l1, o1, qt, from_prev, from_next,
                gp, gn, attn, dos1, delta1, dq2,
-               kh, vh, regh, s_ref, p_ref, ds_ref, dk, dv):
+               kh, vh, regh, s_ref, p_ref, ds_ref, dk, dv, don):
+    x = place[1]
+    for k, ref in enumerate((d0, d1, d2, d3)):
+        don[lax.rem(x - k + GROUP, GROUP)] = ref[...].astype(F32).T
     for ref, cols in ((from_prev, slice(0, HALO)), (from_next, slice(HALO, 2 * HALO))):
         kh[:, cols] = ref[:HD, :]
         vh[:, cols] = ref[HD : 2 * HD, :]
@@ -295,7 +312,7 @@
     stat = ((GROUP, TOK, 1), F32)
     wide = ((GROUP, TOK, HD), F32)
     flat = ((HD, ROW), BF)
-    outs = [((ROW, ROW), BF), stat, stat, wide, ((GROUP, TOK, HD), BF), wide, flat, flat, flat]
+    outs = [((ROW, ROW), BF), stat, stat, wide, ((GROUP, TOK, HD), BF), flat, flat, flat]
     outs = outs + [((16, ROW), F32), ((GROUP, 16, 2 * HALO), F32)]
     return call(
         own_forward_kernel, outs, [place, *parts],
@@ -317,6 +334,7 @@
         pltpu.VMEM((GROUP, TOK, HALO), BF),
         pltpu.VMEM((HD, 2 * HALO), F32),
         pltpu.VMEM((HD, 2 * HALO), F32),
+        pltpu.VMEM((GROUP, TOK, HD), F32),
     ]
     return call(
         far_kernel, outs, [place, *ins], scratch, mib=28, out_spaces="f" * len(outs),
@@ -332,7 +350,7 @@
     )
 
 
-def combine_kernel(place, attn, dq, own, from_next, from_prev, full, c0, c1, c2, c3):
+def combine_kernel(place, attn, dq, own, from_next, from_prev, full, c0, c1, c2, c3, stage, sem):
     x = place[1]
     full[:HD, :] = attn[...]
     full[HD : 2 * HD, :] = dq[...]
@@ -340,15 +358,19 @@
     middle = own[:, TOK:HALO] + from_next[:, : HALO - TOK].astype(F32)
     full[2 * HD :, TOK:HALO] = (middle + from_prev[:, TOK:].astype(F32)).astype(BF)
     full[2 * HD :, HALO:] = (own[:, HALO:] + from_next[:, HALO - TOK :].astype(F32)).astype(BF)
-    for k, out in enumerate((c0, c1, c2, c3)):
+    for k, out in enumerate((stage, c1, c2, c3)):
         at = pl.multiple_of(lax.rem(x + k, GROUP) * TOK, TOK)
         out[...] = full[:, pl.ds(at, TOK)]
+        if k == 0:
+            copy = pltpu.make_async_copy(stage, c0, sem)
+            copy.start()
+    copy.wait()
 
 
 def weights_kernel(scale, place, values, gathered, out, tokens, cotangent, sems):
     parts, _, part_rows, _ = gathered.shape
     copies = []
-    for which, into in ((0, tokens), (1, cotangent)):
+    for which, into in ((1, cotangent), (0, tokens)):
         for n in range(parts):
             to = into.at[n * part_rows : (n + 1) * part_rows]
             copies.append(pltpu.make_async_copy(gathered.at[n, which], to, sems.at[which, n]))
@@ -356,10 +378,10 @@
         copy.start()
     for copy in copies[:parts]:
         copy.wait()
-    grads = dot_nn(values[HD:, :], tokens[...])
+    first = dot_nn(values[:HD, :], cotangent[...])
     for copy in copies[parts:]:
         copy.wait()
-    total = (jnp.concatenate([dot_nn(values[:HD, :], cotangent[...]), grads], axis=0) * scale).T
+    total = (jnp.concatenate([first, dot_nn(values[HD:, :], tokens[...])], axis=0) * scale).T
     count = out.shape[0]
     rows = total.shape[0] // (2 * count)
     for z in range(count):
@@ -393,17 +415,23 @@
             grad_qkv[part, :, cols] = piece[:, (part + 1) * HD : (part + 2) * HD]
 
 
-def share_kernel(place, *refs):
-    ins, (w_out, w, send, keep, attn, grads, whole) = refs[:GROUP], refs[GROUP:]
+def share_kernel(place, mine, r1, r2, r3, w_out, w, send, keep, attn, grads, whole, mv, wov, wv, sems):
+    pairs = ((mine, mv), (w_out, wov), (w, wv))
+    copies = [pltpu.make_async_copy(a, b, sems.at[n]) for n, (a, b) in enumerate(pairs)]
+    for copy in copies:
+        copy.start()
     x = place[1]
     core = place[3]
-    for k in range(GROUP):
-        head = lax.rem(x - k + GROUP, GROUP)
-        attn[head] = ins[k][:HD, :]
+    for k, ref in enumerate((r1, r2, r3, mv)):
+        if ref is mv:
+            copies[0].wait()
+        head = lax.rem(x - (k + 1) + GROUP, GROUP)
+        attn[head] = ref[:HD, :]
         for part in range(3):
-            grads[part, head] = ins[k][(part + 1) * HD : (part + 2) * HD, :]
+            grads[part, head] = ref[(part + 1) * HD : (part + 2) * HD, :]
     local = GROUP * HD
-    for n, (weights, held) in enumerate(((w_out, attn), (w, grads))):
+    for n, (weights, held) in enumerate(((wov, attn), (wv, grads))):
+        copies[n + 1].wait()
         values = held[...].reshape(-1, TOK)
         whole[...] = dot_tn(weights[...], values)
         for other, out in ((1, send), (0, keep)):
@@ -435,8 +463,12 @@
             pltpu.VMEM((GROUP, HD, TOK), BF),
             pltpu.VMEM((3, GROUP, HD, TOK), BF),
             pltpu.VMEM((model, TOK), F32),
+            pltpu.VMEM((4 * HD, TOK), BF),
+            pltpu.VMEM(w_out.shape, BF),
+            pltpu.VMEM(w.shape, BF),
+            pltpu.SemaphoreType.DMA((3,)),
         ],
-        mib=16, out_spaces="ff",
+        mib=18, spaces="shfffhh", out_spaces="ff",
     )
     got = shift(send, "c", 1)
     return call(
@@ -455,44 +487,58 @@
     grad_scale = (width * lax.axis_size(SEQ_AXES)) ** (-0.5)
     w2 = w_qkv.transpose(1, 2, 0).reshape(3 * local, model)
 
-    *sent, parts_mine = call(
+    (parts_mine,) = call(
+        halves_kernel, [((2, width // 2, model), BF)], [place, tokens, cotangent],
+        [pltpu.VMEM((2, width // 2, model), BF), pltpu.SemaphoreType.DMA((4,))],
+        spaces="shh", out_spaces="h", moved=4_000_000,
+    )
+    first, parts_mine = lax.optimization_barrier((tokens, parts_mine))
+    sent = call(
         project_kernel,
-        [((SENT, width), BF)] * GROUP + [((2, width // 2, model), BF)],
-        [place, w2, tokens, w_out, cotangent, regions, block_mask],
+        [((SENT, width), BF)] * GROUP,
+        [place, w2, first, regions, block_mask],
         [
-            pltpu.VMEM((3 * local, model), BF),
-            pltpu.VMEM((width, model), BF),
-            pltpu.VMEM((local, model), BF),
+            pltpu.VMEM((3, local, model), BF),
             pltpu.VMEM((width, model), BF),
             pltpu.VMEM(regions.shape, jnp.int32),
             pltpu.VMEM(block_mask.shape, jnp.int32),
             pltpu.VMEM((16, width), F32),
-            pltpu.VMEM((4, GROUP, HD, width), BF),
+            pltpu.VMEM((3, GROUP, HD, width), BF),
             pltpu.VMEM((GROUP, SENT, width), BF),
             pltpu.SemaphoreType.DMA((12,)),
         ],
-        mib=16, spaces="shhhhhh", out_spaces="fhhhh",
-        flops=2 * 4 * local * model * width, moved=8_000_000,
+        mib=16, spaces="shhhh", out_spaces="fhhh",
+        flops=2 * 3 * local * model * width, moved=8_000_000,
     )
     parts = [sent[0]] + [shift(sent[k], "x", k) for k in (1, 2, 3)]
     gathered = lax.all_gather(parts_mine, ("x", "c"), axis=0)
     to_next, to_prev = call(
         halo_kernel, [((2 * HD + 16, HALO), BF)] * 2, [place, *parts], moved=2_000_000
     )
+    late_cot, _ = lax.optimization_barrier((cotangent, sent[0]))
+    sent_grad = call(
+        project_grad_kernel, [((HD, width), BF)] * GROUP, [place, w_out, late_cot],
+        [pltpu.VMEM((GROUP, HD, width), BF)], out_spaces="ffff",
+        flops=2 * local * model * width, moved=3_000_000,
+    )
+    to_next, sent_grad = lax.optimization_barrier((to_next, sent_grad))
+    grads = [sent_grad[0]] + [shift(sent_grad[k], "x", k) for k in (1, 2, 3)]
     from_prev = shift(to_next, ROW_AXES, 1)
     from_next = shift(to_prev, ROW_AXES, -1)
     held = own_forward(place, parts)
-    p1, m1, l1, o1, qn, don, qt, kt, vt, reg, eff_far = held
+    p1, m1, l1, o1, qn, qt, kt, vt, reg, eff_far = held
 
     gp, gn, attn, dos1, delta1, dq2 = far_part(
-        place, [eff_far, reg, qn, don, m1, l1, o1, qt, from_prev, from_next]
+        place, [*grads, eff_far, reg, qn, m1, l1, o1, qt, from_prev, from_next]
     )
     back_next = shift(gp, ROW_AXES, -1)
     back_prev = shift(gn, ROW_AXES, 1)
     dq, own = own_backward(place, [p1, dos1, delta1, dq2, qt, kt, vt])
     d_all, *chunks = call(
         combine_kernel, [((4 * HD, ROW), BF)] + [((4 * HD, width), BF)] * GROUP,
-        [place, attn, dq, own, back_next, back_prev], out_spaces="f" * 5,
+        [place, attn, dq, own, back_next, back_prev],
+        [pltpu.VMEM((4 * HD, width), BF), pltpu.SemaphoreType.DMA],
+        out_spaces="fhfff",
     )
     kv_all = [chunks[0]] + [shift(chunks[k], "x", k) for k in (1, 2, 3)]
     share = model // ROWS // GROUP

time: 129 us -> 126 us (0.977)
  waiting for transfers between devices: 37.9 us -> 31.4 us
  starting transfers between devices: 30.7 us -> 34.6 us
  local copies, waits for them, and re-layouts: 2.87 us -> 0.1 us
  Pallas kernels: 43.5 us -> 45.1 us
    ppermute x12 -> x15, waiting for transfers between devices: 20.7 us -> 13.7 us  [shift(): lax.ppermute(value, axis, [(i, (i + steps) % count) for i in range(count)])]
    ppermute x12 -> x15, starting transfers between devices: 23.7 us -> 27.6 us  [shift(): lax.ppermute(value, axis, [(i, (i + steps) % count) for i in range(count)])]
    unnamed x8 -> x4, local copies, waits for them, and re-layouts: 2.78 us -> 0.01 us
    pallas_call x12 -> x14, Pallas kernels: 43.5 us -> 45.1 us  [call(): pl.pallas_call(kernel, out_shape=[kept.get(c, jax.ShapeDtypeStruct)(s, d)...]
  transfers between devices with their start and end apart: 15 -> 18, of which waited for: 8 -> 7; matrix products, arithmetic and copies ran while one was open for 0% -> 0% of each run, Pallas kernels for 28% -> 33%
where the time goes in v2:
time: 126 us; the launch traced here: 125 us
  Pallas kernels  45.1 us (36%)
  starting transfers between devices  34.6 us (27%)
  waiting for transfers between devices  31.4 us (25%)
  between operations  14.2 us (11%)
    pallas_call x14, Pallas kernels, call(): pl.pallas_call(kernel, out_shape=[kept.get(c, jax.ShapeDtypeStruct)(s, d)...  45.1 us
    ppermute x15, starting transfers between devices, shift(): lax.ppermute(value, axis, [(i, (i + steps) % count) for i in range(count)])  27.6 us
    ppermute x15, waiting for transfers between devices, shift(): lax.ppermute(value, axis, [(i, (i + steps) % count) for i in range(count)])  13.7 us
    all_to_all x1, waiting for transfers between devices, on_device(): spread = lax.all_to_all(terms, 'z', 0, 0, tiled=True)  11.7 us
    all_to_all x1, waiting for transfers between devices, on_device(): final = lax.all_to_all(summed, ('y', 'x'), 0, 0, tiled=True)  6.01 us
    all_to_all x1, starting transfers between devices, on_device(): spread = lax.all_to_all(terms, 'z', 0, 0, tiled=True)  3.56 us
    all_to_all x1, starting transfers between devices, on_device(): final = lax.all_to_all(summed, ('y', 'x'), 0, 0, tiled=True)  3.42 us
  transfers between devices with their start and end apart: 18, of which 7 were waited for; matrix products, arithmetic and copies ran while one was open for 0% of the time, Pallas kernels for 33%

profile of v2, /device:TPU:16, one launch (start us, length us, event | category | flops | bytes accessed | tf_op | source)
XLA Modules:
  0.0 125.4 jit_solution(15306696074185443607)
XLA Ops:
  7.3 2.6 %shard_map.93 = bf16[2,192,1280]{2,1,0:T(8,128)(2,1)} custom-call(s32[5]{0:T(128)S(1)} %stack.23.place, bf16[384,1280]{1,0:T(8,128)(2,1)} %tokens.2, bf16[384,1280]{1,0:T(8,128)(2,1)} %cotangent.2), custom_call_target="tpu_custom_call" | custom-call | bytes 4000000 | tf_op jit(solution)/shard_map/pallas_call | solution.py:57
  10.0 4.8 %shard_map.94 = (bf16[256,384]{1,0:T(8,128)(2,1)S(1)}, bf16[256,384]{1,0:T(8,128)(2,1)}, bf16[256,384]{1,0:T(8,128)(2,1)}, bf16[256,384]{1,0:T(8,128)(2,1)}) custom-call(s32[5]{0:T(128)S(1)} %stack.23.place, bf16[960,1280]{1,0:T(8,128)(2,1)} %bitcast.14, bf16[384,1280]{1,0:T(8,128)(2,1)} %tokens.2, s32[384]{0:T(512)} %regions.1, s32[3,192]{1,0:T(4,128)} %mask.1), custom_call_target="tpu_custom_call" | custom-call | flops 943718400 | bytes 8000000 | tf_op jit(solution)/shard_map/pallas_call | solution.py:57
  14.8 1.6 %collective-permute-start = (bf16[256,384]{1,0:T(8,128)(2,1)}, bf16[256,384]{1,0:T(8,128)(2,1)S(1)}, u32[]{:S(2)}, u32[]{:S(2)}) collective-permute-start(bf16[256,384]{1,0:T(8,128)(2,1)} %get-tuple-element.60), channel_id=1, source_target_pairs={{0,4},{4,8},{8,12},{12,0},{1,5},{5,9},{9,13},{13,1},{2,6},{6,10},{... | collective-permute-start | bytes 589832 | tf_op jit(solution)/shard_map/ppermute | solution.py:39
  16.4 2.7 %collective-permute-start.1 = (bf16[256,384]{1,0:T(8,128)(2,1)}, bf16[256,384]{1,0:T(8,128)(2,1)S(1)}, u32[]{:S(2)}, u32[]{:S(2)}) collective-permute-start(bf16[256,384]{1,0:T(8,128)(2,1)} %get-tuple-element.61), channel_id=1, source_target_pairs={{0,8},{4,12},{8,0},{12,4},{1,9},{5,13},{9,1},{13,5},{2,10},{6,14},... | collective-permute-start | bytes 589832 | tf_op jit(solution)/shard_map/ppermute | solution.py:39
  19.1 1.4 %collective-permute-start.2 = (bf16[256,384]{1,0:T(8,128)(2,1)}, bf16[256,384]{1,0:T(8,128)(2,1)S(1)}, u32[]{:S(2)}, u32[]{:S(2)}) collective-permute-start(bf16[256,384]{1,0:T(8,128)(2,1)} %get-tuple-element.62), channel_id=1, source_target_pairs={{0,12},{4,0},{8,4},{12,8},{1,13},{5,1},{9,5},{13,9},{2,14},{6,2},{... | collective-permute-start | bytes 589832 | tf_op jit(solution)/shard_map/ppermute | solution.py:39
  20.5 1.2 shard_map.96
  21.7 1.4 %collective-permute-done.r1 = bf16[256,384]{1,0:T(8,128)(2,1)S(1)} collective-permute-done((bf16[256,384]{1,0:T(8,128)(2,1)}, bf16[256,384]{1,0:T(8,128)(2,1)S(1)}, u32[]{:S(2)}, u32[]{:S(2)}) %collective-permute-start) | collective-permute-done | bytes 196640 | tf_op jit(solution)/shard_map/ppermute | solution.py:39
  23.1 5.0 %collective-permute-done.1.r2 = bf16[256,384]{1,0:T(8,128)(2,1)S(1)} collective-permute-done((bf16[256,384]{1,0:T(8,128)(2,1)}, bf16[256,384]{1,0:T(8,128)(2,1)S(1)}, u32[]{:S(2)}, u32[]{:S(2)}) %collective-permute-start.1) | collective-permute-done | bytes 196640 | tf_op jit(solution)/shard_map/ppermute | solution.py:39
  28.8 2.0 %collective-permute-start.6 = (bf16[176,1152]{1,0:T(8,128)(2,1)S(1)}, bf16[176,1152]{1,0:T(8,128)(2,1)S(1)}, u32[]{:S(2)}, u32[]{:S(2)}) collective-permute-start(bf16[176,1152]{1,0:T(8,128)(2,1)S(1)} %get-tuple-element.80), channel_id=1, source_target_pairs={{0,16},{16,32},{32,48},{48,64},{64,80},{80,96},{96,112},{112,128},... | collective-permute-start | bytes 1216520 | tf_op jit(solution)/shard_map/ppermute | solution.py:39
  30.8 7.1 %collective-permute-start.7 = (bf16[176,1152]{1,0:T(8,128)(2,1)S(1)}, bf16[176,1152]{1,0:T(8,128)(2,1)S(1)}, u32[]{:S(2)}, u32[]{:S(2)}) collective-permute-start(bf16[176,1152]{1,0:T(8,128)(2,1)S(1)} %get-tuple-element.81), channel_id=1, source_target_pairs={{0,240},{16,0},{32,16},{48,32},{64,48},{80,64},{96,80},{112,96},{1... | collective-permute-start | bytes 1216520 | tf_op jit(solution)/shard_map/ppermute | solution.py:39
  37.9 1.4 %collective-permute-start.3 = (bf16[80,384]{1,0:T(8,128)(2,1)S(1)}, bf16[80,384]{1,0:T(8,128)(2,1)S(1)}, u32[]{:S(2)}, u32[]{:S(2)}) collective-permute-start(bf16[80,384]{1,0:T(8,128)(2,1)S(1)} %get-tuple-element.70), channel_id=1, source_target_pairs={{0,4},{4,8},{8,12},{12,0},{1,5},{5,9},{9,13},{13,1},{2,6},{6,10},{... | collective-permute-start | bytes 184328 | tf_op jit(solution)/shard_map/ppermute | solution.py:39
  39.3 2.6 %collective-permute-start.4 = (bf16[80,384]{1,0:T(8,128)(2,1)S(1)}, bf16[80,384]{1,0:T(8,128)(2,1)S(1)}, u32[]{:S(2)}, u32[]{:S(2)}) collective-permute-start(bf16[80,384]{1,0:T(8,128)(2,1)S(1)} %get-tuple-element.71), channel_id=1, source_target_pairs={{0,8},{4,12},{8,0},{12,4},{1,9},{5,13},{9,1},{13,5},{2,10},{6,14},... | collective-permute-start | bytes 184328 | tf_op jit(solution)/shard_map/ppermute | solution.py:39
  41.9 2.0 %collective-permute-start.5 = (bf16[80,384]{1,0:T(8,128)(2,1)S(1)}, bf16[80,384]{1,0:T(8,128)(2,1)S(1)}, u32[]{:S(2)}, u32[]{:S(2)}) collective-permute-start(bf16[80,384]{1,0:T(8,128)(2,1)S(1)} %get-tuple-element.72), channel_id=1, source_target_pairs={{0,12},{4,0},{8,4},{12,8},{1,13},{5,1},{9,5},{13,9},{2,14},{6,2},{... | collective-permute-start | bytes 184328 | tf_op jit(solution)/shard_map/ppermute | solution.py:39
  44.0 5.8 %shard_map.97 = (bf16[1536,1536]{1,0:T(8,128)(2,1)S(1)}, f32[4,384,1]{2,1,0:T(8,128)S(1)}, f32[4,384,1]{2,1,0:T(8,128)S(1)}, f32[4,384,80]{2,1,0:T(8,128)S(1)}, ...) custom-call(s32[5]{0:T(128)S(1)} %stack.23.place, ...), custom_call_target="tpu_custom_call" | custom-call | flops 1207959552 | bytes 6000000 | tf_op jit(solution)/shard_map/pallas_call | solution.py:57
  49.9 7.9 %shard_map.98 = (bf16[160,1152]{1,0:T(8,128)(2,1)S(1)}, bf16[160,1152]{1,0:T(8,128)(2,1)S(1)}, bf16[80,1536]{1,0:T(8,128)(2,1)S(1)}, bf16[1536,80]{1,0:T(8,128)(...) custom-call(s32[5]{0:T(128)S(1)} %stack.23.place, bf16[80,384]{1,0:T(8,128)(2,1)S(1)} %get-tuple-element.69.d0, ...), custom_call_target="tpu_custom_call" | custom-call | flops 2717908992 | bytes 6000000 | tf_op jit(solution)/shard_map/pallas_call | solution.py:57
  57.8 2.2 %collective-permute-start.8 = (bf16[160,1152]{1,0:T(8,128)(2,1)S(1)}, bf16[160,1152]{1,0:T(8,128)(2,1)S(1)}, u32[]{:S(2)}, u32[]{:S(2)}) collective-permute-start(bf16[160,1152]{1,0:T(8,128)(2,1)S(1)} %get-tuple-element.91), channel_id=1, source_target_pairs={{0,240},{16,0},{32,16},{48,32},{64,48},{80,64},{96,80},{112,96},{1... | collective-permute-start | bytes 1105928 | tf_op jit(solution)/shard_map/ppermute | solution.py:39
  60.1 4.9 %shard_map.99 = (bf16[80,1536]{1,0:T(8,128)(2,1)S(1)}, f32[160,1536]{1,0:T(8,128)S(1)}) custom-call(s32[5]{0:T(128)S(1)} %stack.23.place, bf16[1536,1536]{1,0:T(8,128)(2,1)S(1)} %get-tuple-element.83.p1, bf16[1536,80]{1,0:T(8,128)(2,1)S(1)} %get-tuple-element.84.dos1, f32[4,384,1]{2,1,0:T(8,128)S(1)} %get-tuple-element.85.delta1, ...), custom_call_target="tpu_custom_call" | custom-call | flops 2415919104 | bytes 6000000 | tf_op jit(solution)/shard_map/pallas_call | solution.py:57
  65.6 4.1 %collective-permute-done.9.from_prev = bf16[160,1152]{1,0:T(8,128)(2,1)S(1)} collective-permute-done((bf16[160,1152]{1,0:T(8,128)(2,1)S(1)}, bf16[160,1152]{1,0:T(8,128)(2,1)S(1)}, u32[]{:S(2)}, u32[]{:S(2)}) %collective-permute-start.9) | collective-permute-done | bytes 368672 | tf_op jit(solution)/shard_map/ppermute | solution.py:39
  69.6 1.5 %shard_map.100 = (bf16[320,1536]{1,0:T(8,128)(2,1)S(1)}, bf16[320,384]{1,0:T(8,128)(2,1)}, bf16[320,384]{1,0:T(8,128)(2,1)S(1)}, bf16[320,384]{1,0:T(8,128)(2,1)S(1)}, bf16[320,384]{1,0:T(8,128)(2,1)S(1)}) custom-call(s32[5]{0:T(128)S(1)} %stack.23.place, bf16[80,1536]{1,0:T(8,128)(2,1)S(1)} %get-tuple-element.82.attn, ...), custom_call_target="tpu_custom_call" | custom-call | tf_op jit(solution)/shard_map/pallas_call | solution.py:57
  71.3 2.8 %collective-permute-start.11 = (bf16[320,384]{1,0:T(8,128)(2,1)S(1)}, bf16[320,384]{1,0:T(8,128)(2,1)S(1)}, u32[]{:S(2)}, u32[]{:S(2)}) collective-permute-start(bf16[320,384]{1,0:T(8,128)(2,1)S(1)} %get-tuple-element.98), channel_id=1, source_target_pairs={{0,8},{4,12},{8,0},{12,4},{1,9},{5,13},{9,1},{13,5},{2,10},{6,14},... | collective-permute-start | bytes 737288 | tf_op jit(solution)/shard_map/ppermute | solution.py:39
  74.2 0.7 collective-permute-start.12
  74.9 6.2 %shard_map.101 = bf16[8,208,256]{2,1,0:T(8,128)(2,1)} custom-call(s32[5]{0:T(128)S(1)} %stack.23.place, bf16[320,1536]{1,0:T(8,128)(2,1)S(1)} %get-tuple-element.94.values, bf16[8,2,192,1280]{3,2,1,0:T(8,128)(2,1)} %bitcast.13), custom_call_target="tpu_custom_call" | custom-call | tf_op jit(solution)/shard_map/pallas_call | solution.py:57
  81.1 3.6 %all-to-all-start = ((bf16[8,208,256]{2,1,0:T(8,128)(2,1)}), bf16[8,208,256]{2,1,0:T(8,128)(2,1)S(1)}, u32[]{:S(2)}, u32[]{:S(2)}) async-start(bf16[8,208,256]{2,1,0:T(8,128)(2,1)} %shard_map.101), calls=%async_computation | async-start | bytes 1703936 | tf_op jit(solution)/shard_map/all_to_all | solution.py:557
  84.7 4.7 %shard_map.103 = (bf16[2,2,320,384]{3,2,1,0:T(8,128)(2,1)S(1)}, f32[2,2,320,384]{3,2,1,0:T(8,128)S(1)}) custom-call(s32[5]{0:T(128)S(1)} %stack.23.place, bf16[320,384]{1,0:T(8,128)(2,1)} %get-tuple-element.96.mine, bf16[320,384]{1,0:T(8,128)(2,1)S(1)} %collective-permute-done.10.r1, bf16[320,384]{1,0:T(8,128)(2,1)S(1)} %collective-permute-done.11.r2, ...), custom_call_target="tpu_custom_call" | custom-call | tf_op jit(solution)/shard_map/pallas_call | solution.py:57
  89.6 2.6 %collective-permute-done.13.got = bf16[2,2,320,384]{3,2,1,0:T(8,128)(2,1)S(1)} collective-permute-done((bf16[2,2,320,384]{3,2,1,0:T(8,128)(2,1)S(1)}, bf16[2,2,320,384]{3,2,1,0:T(8,128)(2,1)S(1)}, u32[]{:S(2)}, u32[]{:S(2)}) %collective-permute-start.13) | collective-permute-done | bytes 983072 | tf_op jit(solution)/shard_map/ppermute | solution.py:39
  92.1 0.7 shard_map.104
  93.3 11.7 %all-to-all-done.spread = bf16[8,208,256]{2,1,0:T(8,128)(2,1)S(1)} async-done(((bf16[8,208,256]{2,1,0:T(8,128)(2,1)}), bf16[8,208,256]{2,1,0:T(8,128)(2,1)S(1)}, u32[]{:S(2)}, u32[]{:S(2)}) %all-to-all-start) | async-done | bytes 852000 | tf_op jit(solution)/shard_map/all_to_all | solution.py:557
  105.0 1.4 %shard_map.102 = f32[8,20,320]{2,1,0:T(8,128)} custom-call(s32[5]{0:T(128)S(1)} %stack.23.place, bf16[8,208,256]{2,1,0:T(8,128)(2,1)S(1)} %all-to-all-done.spread), custom_call_target="tpu_custom_call" | custom-call | tf_op jit(solution)/shard_map/pallas_call | solution.py:57
  106.4 3.4 %all-to-all-start.1 = ((f32[8,20,320]{2,1,0:T(8,128)}), f32[8,20,320]{2,1,0:T(8,128)S(1)}, u32[]{:S(2)}, u32[]{:S(2)}) async-start(f32[8,20,320]{2,1,0:T(8,128)} %shard_map.102), calls=%async_computation.1 | async-start | bytes 589824 | tf_op jit(solution)/shard_map/all_to_all | solution.py:561
  109.9 1.4 %shard_map.105 = (bf16[320,384]{1,0:T(8,128)(2,1)}, bf16[320,384]{1,0:T(8,128)(2,1)}) custom-call(s32[5]{0:T(128)S(1)} %stack.23.place, f32[2,320,384]{2,1,0:T(8,128)S(1)} %get-tuple-element.102.mine, bf16[2,320,384]{2,1,0:T(8,128)(2,1)S(1)} %collective-permute-done.14.got), custom_call_target="tpu_custom_call" | custom-call | tf_op jit(solution)/shard_map/pallas_call | solution.py:57
  111.3 6.0 %all-to-all-done.1.final = f32[8,20,320]{2,1,0:T(8,128)S(1)} async-done(((f32[8,20,320]{2,1,0:T(8,128)}), f32[8,20,320]{2,1,0:T(8,128)S(1)}, u32[]{:S(2)}, u32[]{:S(2)}) %all-to-all-start.1) | async-done | bytes 204832 | tf_op jit(solution)/shard_map/all_to_all | solution.py:561
  117.3 1.3 %shard_map.106 = (f32[3,20,320]{2,1,0:T(8,128)}, f32[20,320]{1,0:T(8,128)}) custom-call(s32[5]{0:T(128)S(1)} %stack.23.place, f32[8,20,320]{2,1,0:T(8,128)S(1)} %all-to-all-done.1.final), custom_call_target="tpu_custom_call" | custom-call | tf_op jit(solution)/shard_map/pallas_call | solution.py:57
  (24 shorter events, 2.4 us)
Async XLA Ops:
  7.2 13.4 %copy-start = (bf16[384,1280]{1,0:T(8,128)(2,1)S(1)}, bf16[384,1280]{1,0:T(8,128)(2,1)}, u32[]{:S(2)}) copy-start(bf16[384,1280]{1,0:T(8,128)(2,1)} %cotangent.2) | copy-start | bytes 2949124
  7.2 13.4 %copy-start.1 = (bf16[320,1280]{1,0:T(8,128)(2,1)S(1)}, bf16[320,1280]{1,0:T(8,128)(2,1)}, u32[]{:S(2)}) copy-start(bf16[320,1280]{1,0:T(8,128)(2,1)} %w_out.3) | copy-start | bytes 2457604
  7.2 67.7 %all-gather.3.cloned.1.call-start = ((), (), s32[]{:S(2)}) async-start(), calls=%async_computation.2 | async-start | bytes 8847360 | tf_op jit(solution)/shard_map/all_gather | solution.py:514
  14.8 8.3 %collective-permute-start = (bf16[256,384]{1,0:T(8,128)(2,1)}, bf16[256,384]{1,0:T(8,128)(2,1)S(1)}, u32[]{:S(2)}, u32[]{:S(2)}) collective-permute-start(bf16[256,384]{1,0:T(8,128)(2,1)} %get-tuple-element.60), channel_id=1, source_target_pairs={{0,4},{4,8},{8,12},{12,0},{1,5},{5,9},{9,13},{13,1},{2,6},{6,10},{... | collective-permute-start | bytes 589832 | tf_op jit(solution)/shard_map/ppermute | solution.py:39
  16.4 11.8 %collective-permute-start.1 = (bf16[256,384]{1,0:T(8,128)(2,1)}, bf16[256,384]{1,0:T(8,128)(2,1)S(1)}, u32[]{:S(2)}, u32[]{:S(2)}) collective-permute-start(bf16[256,384]{1,0:T(8,128)(2,1)} %get-tuple-element.61), channel_id=1, source_target_pairs={{0,8},{4,12},{8,0},{12,4},{1,9},{5,13},{9,1},{13,5},{2,10},{6,14},... | collective-permute-start | bytes 589832 | tf_op jit(solution)/shard_map/ppermute | solution.py:39
  19.1 9.0 %collective-permute-start.2 = (bf16[256,384]{1,0:T(8,128)(2,1)}, bf16[256,384]{1,0:T(8,128)(2,1)S(1)}, u32[]{:S(2)}, u32[]{:S(2)}) collective-permute-start(bf16[256,384]{1,0:T(8,128)(2,1)} %get-tuple-element.62), channel_id=1, source_target_pairs={{0,12},{4,0},{8,4},{12,8},{1,13},{5,1},{9,5},{13,9},{2,14},{6,2},{... | collective-permute-start | bytes 589832 | tf_op jit(solution)/shard_map/ppermute | solution.py:39
  28.8 21.0 %collective-permute-start.6 = (bf16[176,1152]{1,0:T(8,128)(2,1)S(1)}, bf16[176,1152]{1,0:T(8,128)(2,1)S(1)}, u32[]{:S(2)}, u32[]{:S(2)}) collective-permute-start(bf16[176,1152]{1,0:T(8,128)(2,1)S(1)} %get-tuple-element.80), channel_id=1, source_target_pairs={{0,16},{16,32},{32,48},{48,64},{64,80},{80,96},{96,112},{112,128},... | collective-permute-start | bytes 1216520 | tf_op jit(solution)/shard_map/ppermute | solution.py:39
  30.8 19.0 %collective-permute-start.7 = (bf16[176,1152]{1,0:T(8,128)(2,1)S(1)}, bf16[176,1152]{1,0:T(8,128)(2,1)S(1)}, u32[]{:S(2)}, u32[]{:S(2)}) collective-permute-start(bf16[176,1152]{1,0:T(8,128)(2,1)S(1)} %get-tuple-element.81), channel_id=1, source_target_pairs={{0,240},{16,0},{32,16},{48,32},{64,48},{80,64},{96,80},{112,96},{1... | collective-permute-start | bytes 1216520 | tf_op jit(solution)/shard_map/ppermute | solution.py:39
  37.9 11.9 %collective-permute-start.3 = (bf16[80,384]{1,0:T(8,128)(2,1)S(1)}, bf16[80,384]{1,0:T(8,128)(2,1)S(1)}, u32[]{:S(2)}, u32[]{:S(2)}) collective-permute-start(bf16[80,384]{1,0:T(8,128)(2,1)S(1)} %get-tuple-element.70), channel_id=1, source_target_pairs={{0,4},{4,8},{8,12},{12,0},{1,5},{5,9},{9,13},{13,1},{2,6},{6,10},{... | collective-permute-start | bytes 184328 | tf_op jit(solution)/shard_map/ppermute | solution.py:39
  39.3 10.5 %collective-permute-start.4 = (bf16[80,384]{1,0:T(8,128)(2,1)S(1)}, bf16[80,384]{1,0:T(8,128)(2,1)S(1)}, u32[]{:S(2)}, u32[]{:S(2)}) collective-permute-start(bf16[80,384]{1,0:T(8,128)(2,1)S(1)} %get-tuple-element.71), channel_id=1, source_target_pairs={{0,8},{4,12},{8,0},{12,4},{1,9},{5,13},{9,1},{13,5},{2,10},{6,14},... | collective-permute-start | bytes 184328 | tf_op jit(solution)/shard_map/ppermute | solution.py:39
  41.9 7.9 %collective-permute-start.5 = (bf16[80,384]{1,0:T(8,128)(2,1)S(1)}, bf16[80,384]{1,0:T(8,128)(2,1)S(1)}, u32[]{:S(2)}, u32[]{:S(2)}) collective-permute-start(bf16[80,384]{1,0:T(8,128)(2,1)S(1)} %get-tuple-element.72), channel_id=1, source_target_pairs={{0,12},{4,0},{8,4},{12,8},{1,13},{5,1},{9,5},{13,9},{2,14},{6,2},{... | collective-permute-start | bytes 184328 | tf_op jit(solution)/shard_map/ppermute | solution.py:39
  57.8 7.8 %collective-permute-start.8 = (bf16[160,1152]{1,0:T(8,128)(2,1)S(1)}, bf16[160,1152]{1,0:T(8,128)(2,1)S(1)}, u32[]{:S(2)}, u32[]{:S(2)}) collective-permute-start(bf16[160,1152]{1,0:T(8,128)(2,1)S(1)} %get-tuple-element.91), channel_id=1, source_target_pairs={{0,240},{16,0},{32,16},{48,32},{64,48},{80,64},{96,80},{112,96},{1... | collective-permute-start | bytes 1105928 | tf_op jit(solution)/shard_map/ppermute | solution.py:39
  60.0 9.6 %collective-permute-start.9 = (bf16[160,1152]{1,0:T(8,128)(2,1)S(1)}, bf16[160,1152]{1,0:T(8,128)(2,1)S(1)}, u32[]{:S(2)}, u32[]{:S(2)}) collective-permute-start(bf16[160,1152]{1,0:T(8,128)(2,1)S(1)} %get-tuple-element.92), channel_id=1, source_target_pairs={{0,16},{16,32},{32,48},{48,64},{64,80},{80,96},{96,112},{112,128},... | collective-permute-start | bytes 1105928 | tf_op jit(solution)/shard_map/ppermute | solution.py:39
  71.1 13.5 %collective-permute-start.10 = (bf16[320,384]{1,0:T(8,128)(2,1)S(1)}, bf16[320,384]{1,0:T(8,128)(2,1)S(1)}, u32[]{:S(2)}, u32[]{:S(2)}) collective-permute-start(bf16[320,384]{1,0:T(8,128)(2,1)S(1)} %get-tuple-element.97), channel_id=1, source_target_pairs={{0,4},{4,8},{8,12},{12,0},{1,5},{5,9},{9,13},{13,1},{2,6},{6,10},{... | collective-permute-start | bytes 737288 | tf_op jit(solution)/shard_map/ppermute | solution.py:39
  71.3 13.4 %collective-permute-start.11 = (bf16[320,384]{1,0:T(8,128)(2,1)S(1)}, bf16[320,384]{1,0:T(8,128)(2,1)S(1)}, u32[]{:S(2)}, u32[]{:S(2)}) collective-permute-start(bf16[320,384]{1,0:T(8,128)(2,1)S(1)} %get-tuple-element.98), channel_id=1, source_target_pairs={{0,8},{4,12},{8,0},{12,4},{1,9},{5,13},{9,1},{13,5},{2,10},{6,14},... | collective-permute-start | bytes 737288 | tf_op jit(solution)/shard_map/ppermute | solution.py:39
  74.2 10.6 %collective-permute-start.12 = (bf16[320,384]{1,0:T(8,128)(2,1)S(1)}, bf16[320,384]{1,0:T(8,128)(2,1)S(1)}, u32[]{:S(2)}, u32[]{:S(2)}) collective-permute-start(bf16[320,384]{1,0:T(8,128)(2,1)S(1)} %get-tuple-element.99), channel_id=1, source_target_pairs={{0,12},{4,0},{8,4},{12,8},{1,13},{5,1},{9,5},{13,9},{2,14},{6,2},{... | collective-permute-start | bytes 737288 | tf_op jit(solution)/shard_map/ppermute | solution.py:39
  81.1 23.9 %all-to-all-start = ((bf16[8,208,256]{2,1,0:T(8,128)(2,1)}), bf16[8,208,256]{2,1,0:T(8,128)(2,1)S(1)}, u32[]{:S(2)}, u32[]{:S(2)}) async-start(bf16[8,208,256]{2,1,0:T(8,128)(2,1)} %shard_map.101), calls=%async_computation | async-start | bytes 1703936 | tf_op jit(solution)/shard_map/all_to_all | solution.py:557
  89.5 2.7 %collective-permute-start.13 = (bf16[2,2,320,384]{3,2,1,0:T(8,128)(2,1)S(1)}, bf16[2,2,320,384]{3,2,1,0:T(8,128)(2,1)S(1)}, u32[]{:S(2)}, u32[]{:S(2)}) collective-permute-start(bf16[2,2,320,384]{3,2,1,0:T(8,128)(2,1)S(1)} %get-tuple-element.101), channel_id=1, source_target_pairs={{0,1},{1,0},{2,3},{3,2},{4,5},{5,4},{6,7},{7,6},{8,9},{9,8},{10,11... | collective-permute-start | bytes 2949128 | tf_op jit(solution)/shard_map/ppermute | solution.py:39
  92.8 17.1 %collective-permute-start.14 = (bf16[2,320,384]{2,1,0:T(8,128)(2,1)S(1)}, bf16[2,320,384]{2,1,0:T(8,128)(2,1)S(1)}, u32[]{:S(2)}, u32[]{:S(2)}) collective-permute-start(bf16[2,320,384]{2,1,0:T(8,128)(2,1)S(1)} %get-tuple-element.103), channel_id=1, source_target_pairs={{0,2},{2,0},{1,3},{3,1},{4,6},{6,4},{5,7},{7,5},{8,10},{10,8},{9,1... | collective-permute-start | bytes 1474568 | tf_op jit(solution)/shard_map/ppermute | solution.py:39
  106.4 10.8 %all-to-all-start.1 = ((f32[8,20,320]{2,1,0:T(8,128)}), f32[8,20,320]{2,1,0:T(8,128)S(1)}, u32[]{:S(2)}, u32[]{:S(2)}) async-start(f32[8,20,320]{2,1,0:T(8,128)} %shard_map.102), calls=%async_computation.1 | async-start | bytes 589824 | tf_op jit(solution)/shard_map/all_to_all | solution.py:561
Sparse Core Ops, SparseCore 0:
  10.1 55.4 all-gather.2

commit v3 on v2

--- a/solution.py
+++ b/solution.py
@@ -402,13 +402,13 @@
     for n in range(count):
         at = rest + (n % 2) * share
         left = (n // 2) * (4 * HD - MAIN)
-        out[n, :, :MAIN] = total[n * share : (n + 1) * share]
-        out[n, :, MAIN:] = total[at : at + share, left : left + 4 * HD - MAIN]
+        out[n, :, :MAIN] = total[n * share : (n + 1) * share].astype(BF)
+        out[n, :, MAIN:] = total[at : at + share, left : left + 4 * HD - MAIN].astype(BF)
 
 
 def order_kernel(place, final, grad_qkv, grad_out):
     for h in range(GROUP):
-        piece = final[h] + final[GROUP + h]
+        piece = final[h].astype(F32) + final[GROUP + h].astype(F32)
         cols = slice(h * HD, (h + 1) * HD)
         grad_out[:, cols] = piece[:, :HD]
         for part in range(3):
@@ -557,7 +557,7 @@
     spread = lax.all_to_all(terms, "z", 0, 0, tiled=True)
     other, mine = scatter_core(place, kv_all, w_out, w2)
     got = shift(other, "h", 1)
-    (summed,) = call(row_sum_kernel, [((2 * GROUP, share, 4 * HD), F32)], [place, spread], out_spaces="f")
+    (summed,) = call(row_sum_kernel, [((2 * GROUP, share, 4 * HD), BF)], [place, spread], out_spaces="f")
     final = lax.all_to_all(summed, ("y", "x"), 0, 0, tiled=True)
     mixed_t, grad_tokens_t = call(head_sum_kernel, [((local, width), BF)] * 2, [place, mine, got])
     final, mixed_t = lax.optimization_barrier((final, mixed_t))

time: 126 us -> 125 us (level)
  no operation moved by 1% of the time
where the time goes in v3:
time: 125 us
  Pallas kernels  45.1 us (36%)
  starting transfers between devices  34.5 us (28%)
  waiting for transfers between devices  30.6 us (24%)
  between operations  14.2 us (11%)
    pallas_call x14, Pallas kernels, call(): pl.pallas_call(kernel, out_shape=[kept.get(c, jax.ShapeDtypeStruct)(s, d)...  45.1 us
    ppermute x15, starting transfers between devices, shift(): lax.ppermute(value, axis, [(i, (i + steps) % count) for i in range(count)])  27.6 us
    ppermute x15, waiting for transfers between devices, shift(): lax.ppermute(value, axis, [(i, (i + steps) % count) for i in range(count)])  13.7 us
    all_to_all x1, waiting for transfers between devices, on_device(): spread = lax.all_to_all(terms, 'z', 0, 0, tiled=True)  11.7 us
    all_to_all x1, waiting for transfers between devices, on_device(): final = lax.all_to_all(summed, ('y', 'x'), 0, 0, tiled=True)  5.25 us
    all_to_all x1, starting transfers between devices, on_device(): spread = lax.all_to_all(terms, 'z', 0, 0, tiled=True)  3.56 us
    all_to_all x1, starting transfers between devices, on_device(): final = lax.all_to_all(summed, ('y', 'x'), 0, 0, tiled=True)  3.38 us
  transfers between devices with their start and end apart: 18, of which 7 were waited for; matrix products, arithmetic and copies ran while one was open for 0% of the time, Pallas kernels for 33%

profile of v3, /device:TPU:16, one launch (start us, length us, event | category | flops | bytes accessed | tf_op | source)
XLA Modules:
  0.0 124.6 jit_solution(17088248687131797728)
XLA Ops:
  7.3 2.6 %shard_map.93 = bf16[2,192,1280]{2,1,0:T(8,128)(2,1)} custom-call(s32[5]{0:T(128)S(1)} %stack.23.place, bf16[384,1280]{1,0:T(8,128)(2,1)} %tokens.2, bf16[384,1280]{1,0:T(8,128)(2,1)} %cotangent.2), custom_call_target="tpu_custom_call" | custom-call | bytes 4000000 | tf_op jit(solution)/shard_map/pallas_call | solution.py:57
  10.0 4.8 %shard_map.94 = (bf16[256,384]{1,0:T(8,128)(2,1)S(1)}, bf16[256,384]{1,0:T(8,128)(2,1)}, bf16[256,384]{1,0:T(8,128)(2,1)}, bf16[256,384]{1,0:T(8,128)(2,1)}) custom-call(s32[5]{0:T(128)S(1)} %stack.23.place, bf16[960,1280]{1,0:T(8,128)(2,1)} %bitcast.14, bf16[384,1280]{1,0:T(8,128)(2,1)} %tokens.2, s32[384]{0:T(512)} %regions.1, s32[3,192]{1,0:T(4,128)} %mask.1), custom_call_target="tpu_custom_call" | custom-call | flops 943718400 | bytes 8000000 | tf_op jit(solution)/shard_map/pallas_call | solution.py:57
  14.8 1.6 %collective-permute-start = (bf16[256,384]{1,0:T(8,128)(2,1)}, bf16[256,384]{1,0:T(8,128)(2,1)S(1)}, u32[]{:S(2)}, u32[]{:S(2)}) collective-permute-start(bf16[256,384]{1,0:T(8,128)(2,1)} %get-tuple-element.60), channel_id=1, source_target_pairs={{0,4},{4,8},{8,12},{12,0},{1,5},{5,9},{9,13},{13,1},{2,6},{6,10},{... | collective-permute-start | bytes 589832 | tf_op jit(solution)/shard_map/ppermute | solution.py:39
  16.4 2.7 %collective-permute-start.1 = (bf16[256,384]{1,0:T(8,128)(2,1)}, bf16[256,384]{1,0:T(8,128)(2,1)S(1)}, u32[]{:S(2)}, u32[]{:S(2)}) collective-permute-start(bf16[256,384]{1,0:T(8,128)(2,1)} %get-tuple-element.61), channel_id=1, source_target_pairs={{0,8},{4,12},{8,0},{12,4},{1,9},{5,13},{9,1},{13,5},{2,10},{6,14},... | collective-permute-start | bytes 589832 | tf_op jit(solution)/shard_map/ppermute | solution.py:39
  19.1 1.4 %collective-permute-start.2 = (bf16[256,384]{1,0:T(8,128)(2,1)}, bf16[256,384]{1,0:T(8,128)(2,1)S(1)}, u32[]{:S(2)}, u32[]{:S(2)}) collective-permute-start(bf16[256,384]{1,0:T(8,128)(2,1)} %get-tuple-element.62), channel_id=1, source_target_pairs={{0,12},{4,0},{8,4},{12,8},{1,13},{5,1},{9,5},{13,9},{2,14},{6,2},{... | collective-permute-start | bytes 589832 | tf_op jit(solution)/shard_map/ppermute | solution.py:39
  20.5 1.2 shard_map.96
  21.7 1.4 %collective-permute-done.r1 = bf16[256,384]{1,0:T(8,128)(2,1)S(1)} collective-permute-done((bf16[256,384]{1,0:T(8,128)(2,1)}, bf16[256,384]{1,0:T(8,128)(2,1)S(1)}, u32[]{:S(2)}, u32[]{:S(2)}) %collective-permute-start) | collective-permute-done | bytes 196640 | tf_op jit(solution)/shard_map/ppermute | solution.py:39
  23.1 5.0 %collective-permute-done.1.r2 = bf16[256,384]{1,0:T(8,128)(2,1)S(1)} collective-permute-done((bf16[256,384]{1,0:T(8,128)(2,1)}, bf16[256,384]{1,0:T(8,128)(2,1)S(1)}, u32[]{:S(2)}, u32[]{:S(2)}) %collective-permute-start.1) | collective-permute-done | bytes 196640 | tf_op jit(solution)/shard_map/ppermute | solution.py:39
  28.8 2.0 %collective-permute-start.6 = (bf16[176,1152]{1,0:T(8,128)(2,1)S(1)}, bf16[176,1152]{1,0:T(8,128)(2,1)S(1)}, u32[]{:S(2)}, u32[]{:S(2)}) collective-permute-start(bf16[176,1152]{1,0:T(8,128)(2,1)S(1)} %get-tuple-element.80), channel_id=1, source_target_pairs={{0,16},{16,32},{32,48},{48,64},{64,80},{80,96},{96,112},{112,128},... | collective-permute-start | bytes 1216520 | tf_op jit(solution)/shard_map/ppermute | solution.py:39
  30.8 7.1 %collective-permute-start.7 = (bf16[176,1152]{1,0:T(8,128)(2,1)S(1)}, bf16[176,1152]{1,0:T(8,128)(2,1)S(1)}, u32[]{:S(2)}, u32[]{:S(2)}) collective-permute-start(bf16[176,1152]{1,0:T(8,128)(2,1)S(1)} %get-tuple-element.81), channel_id=1, source_target_pairs={{0,240},{16,0},{32,16},{48,32},{64,48},{80,64},{96,80},{112,96},{1... | collective-permute-start | bytes 1216520 | tf_op jit(solution)/shard_map/ppermute | solution.py:39
  37.9 1.4 %collective-permute-start.3 = (bf16[80,384]{1,0:T(8,128)(2,1)S(1)}, bf16[80,384]{1,0:T(8,128)(2,1)S(1)}, u32[]{:S(2)}, u32[]{:S(2)}) collective-permute-start(bf16[80,384]{1,0:T(8,128)(2,1)S(1)} %get-tuple-element.70), channel_id=1, source_target_pairs={{0,4},{4,8},{8,12},{12,0},{1,5},{5,9},{9,13},{13,1},{2,6},{6,10},{... | collective-permute-start | bytes 184328 | tf_op jit(solution)/shard_map/ppermute | solution.py:39
  39.3 2.6 %collective-permute-start.4 = (bf16[80,384]{1,0:T(8,128)(2,1)S(1)}, bf16[80,384]{1,0:T(8,128)(2,1)S(1)}, u32[]{:S(2)}, u32[]{:S(2)}) collective-permute-start(bf16[80,384]{1,0:T(8,128)(2,1)S(1)} %get-tuple-element.71), channel_id=1, source_target_pairs={{0,8},{4,12},{8,0},{12,4},{1,9},{5,13},{9,1},{13,5},{2,10},{6,14},... | collective-permute-start | bytes 184328 | tf_op jit(solution)/shard_map/ppermute | solution.py:39
  41.9 2.0 %collective-permute-start.5 = (bf16[80,384]{1,0:T(8,128)(2,1)S(1)}, bf16[80,384]{1,0:T(8,128)(2,1)S(1)}, u32[]{:S(2)}, u32[]{:S(2)}) collective-permute-start(bf16[80,384]{1,0:T(8,128)(2,1)S(1)} %get-tuple-element.72), channel_id=1, source_target_pairs={{0,12},{4,0},{8,4},{12,8},{1,13},{5,1},{9,5},{13,9},{2,14},{6,2},{... | collective-permute-start | bytes 184328 | tf_op jit(solution)/shard_map/ppermute | solution.py:39
  44.0 5.8 %shard_map.97 = (bf16[1536,1536]{1,0:T(8,128)(2,1)S(1)}, f32[4,384,1]{2,1,0:T(8,128)S(1)}, f32[4,384,1]{2,1,0:T(8,128)S(1)}, f32[4,384,80]{2,1,0:T(8,128)S(1)}, ...) custom-call(s32[5]{0:T(128)S(1)} %stack.23.place, ...), custom_call_target="tpu_custom_call" | custom-call | flops 1207959552 | bytes 6000000 | tf_op jit(solution)/shard_map/pallas_call | solution.py:57
  49.9 7.9 %shard_map.98 = (bf16[160,1152]{1,0:T(8,128)(2,1)S(1)}, bf16[160,1152]{1,0:T(8,128)(2,1)S(1)}, bf16[80,1536]{1,0:T(8,128)(2,1)S(1)}, bf16[1536,80]{1,0:T(8,128)(...) custom-call(s32[5]{0:T(128)S(1)} %stack.23.place, bf16[80,384]{1,0:T(8,128)(2,1)S(1)} %get-tuple-element.69.d0, ...), custom_call_target="tpu_custom_call" | custom-call | flops 2717908992 | bytes 6000000 | tf_op jit(solution)/shard_map/pallas_call | solution.py:57
  57.8 2.2 %collective-permute-start.8 = (bf16[160,1152]{1,0:T(8,128)(2,1)S(1)}, bf16[160,1152]{1,0:T(8,128)(2,1)S(1)}, u32[]{:S(2)}, u32[]{:S(2)}) collective-permute-start(bf16[160,1152]{1,0:T(8,128)(2,1)S(1)} %get-tuple-element.91), channel_id=1, source_target_pairs={{0,240},{16,0},{32,16},{48,32},{64,48},{80,64},{96,80},{112,96},{1... | collective-permute-start | bytes 1105928 | tf_op jit(solution)/shard_map/ppermute | solution.py:39
  60.1 4.9 %shard_map.99 = (bf16[80,1536]{1,0:T(8,128)(2,1)S(1)}, f32[160,1536]{1,0:T(8,128)S(1)}) custom-call(s32[5]{0:T(128)S(1)} %stack.23.place, bf16[1536,1536]{1,0:T(8,128)(2,1)S(1)} %get-tuple-element.83.p1, bf16[1536,80]{1,0:T(8,128)(2,1)S(1)} %get-tuple-element.84.dos1, f32[4,384,1]{2,1,0:T(8,128)S(1)} %get-tuple-element.85.delta1, ...), custom_call_target="tpu_custom_call" | custom-call | flops 2415919104 | bytes 6000000 | tf_op jit(solution)/shard_map/pallas_call | solution.py:57
  65.6 4.1 %collective-permute-done.9.from_prev = bf16[160,1152]{1,0:T(8,128)(2,1)S(1)} collective-permute-done((bf16[160,1152]{1,0:T(8,128)(2,1)S(1)}, bf16[160,1152]{1,0:T(8,128)(2,1)S(1)}, u32[]{:S(2)}, u32[]{:S(2)}) %collective-permute-start.9) | collective-permute-done | bytes 368672 | tf_op jit(solution)/shard_map/ppermute | solution.py:39
  69.6 1.5 %shard_map.100 = (bf16[320,1536]{1,0:T(8,128)(2,1)S(1)}, bf16[320,384]{1,0:T(8,128)(2,1)}, bf16[320,384]{1,0:T(8,128)(2,1)S(1)}, bf16[320,384]{1,0:T(8,128)(2,1)S(1)}, bf16[320,384]{1,0:T(8,128)(2,1)S(1)}) custom-call(s32[5]{0:T(128)S(1)} %stack.23.place, bf16[80,1536]{1,0:T(8,128)(2,1)S(1)} %get-tuple-element.82.attn, ...), custom_call_target="tpu_custom_call" | custom-call | tf_op jit(solution)/shard_map/pallas_call | solution.py:57
  71.3 2.8 %collective-permute-start.11 = (bf16[320,384]{1,0:T(8,128)(2,1)S(1)}, bf16[320,384]{1,0:T(8,128)(2,1)S(1)}, u32[]{:S(2)}, u32[]{:S(2)}) collective-permute-start(bf16[320,384]{1,0:T(8,128)(2,1)S(1)} %get-tuple-element.98), channel_id=1, source_target_pairs={{0,8},{4,12},{8,0},{12,4},{1,9},{5,13},{9,1},{13,5},{2,10},{6,14},... | collective-permute-start | bytes 737288 | tf_op jit(solution)/shard_map/ppermute | solution.py:39
  74.2 0.7 collective-permute-start.12
  74.9 6.2 %shard_map.101 = bf16[8,208,256]{2,1,0:T(8,128)(2,1)} custom-call(s32[5]{0:T(128)S(1)} %stack.23.place, bf16[320,1536]{1,0:T(8,128)(2,1)S(1)} %get-tuple-element.94.values, bf16[8,2,192,1280]{3,2,1,0:T(8,128)(2,1)} %bitcast.13), custom_call_target="tpu_custom_call" | custom-call | tf_op jit(solution)/shard_map/pallas_call | solution.py:57
  81.1 3.6 %all-to-all-start = ((bf16[8,208,256]{2,1,0:T(8,128)(2,1)}), bf16[8,208,256]{2,1,0:T(8,128)(2,1)S(1)}, u32[]{:S(2)}, u32[]{:S(2)}) async-start(bf16[8,208,256]{2,1,0:T(8,128)(2,1)} %shard_map.101), calls=%async_computation | async-start | bytes 1703936 | tf_op jit(solution)/shard_map/all_to_all | solution.py:557
  84.7 4.7 %shard_map.103 = (bf16[2,2,320,384]{3,2,1,0:T(8,128)(2,1)S(1)}, f32[2,2,320,384]{3,2,1,0:T(8,128)S(1)}) custom-call(s32[5]{0:T(128)S(1)} %stack.23.place, bf16[320,384]{1,0:T(8,128)(2,1)} %get-tuple-element.96.mine, bf16[320,384]{1,0:T(8,128)(2,1)S(1)} %collective-permute-done.10.r1, bf16[320,384]{1,0:T(8,128)(2,1)S(1)} %collective-permute-done.11.r2, ...), custom_call_target="tpu_custom_call" | custom-call | tf_op jit(solution)/shard_map/pallas_call | solution.py:57
  89.6 2.6 %collective-permute-done.13.got = bf16[2,2,320,384]{3,2,1,0:T(8,128)(2,1)S(1)} collective-permute-done((bf16[2,2,320,384]{3,2,1,0:T(8,128)(2,1)S(1)}, bf16[2,2,320,384]{3,2,1,0:T(8,128)(2,1)S(1)}, u32[]{:S(2)}, u32[]{:S(2)}) %collective-permute-start.13) | collective-permute-done | bytes 983072 | tf_op jit(solution)/shard_map/ppermute | solution.py:39
  92.1 0.7 shard_map.104
  93.3 11.7 %all-to-all-done.spread = bf16[8,208,256]{2,1,0:T(8,128)(2,1)S(1)} async-done(((bf16[8,208,256]{2,1,0:T(8,128)(2,1)}), bf16[8,208,256]{2,1,0:T(8,128)(2,1)S(1)}, u32[]{:S(2)}, u32[]{:S(2)}) %all-to-all-start) | async-done | bytes 852000 | tf_op jit(solution)/shard_map/all_to_all | solution.py:557
  105.0 1.4 %shard_map.102 = bf16[8,20,320]{2,1,0:T(8,128)(2,1)} custom-call(s32[5]{0:T(128)S(1)} %stack.23.place, bf16[8,208,256]{2,1,0:T(8,128)(2,1)S(1)} %all-to-all-done.spread), custom_call_target="tpu_custom_call" | custom-call | tf_op jit(solution)/shard_map/pallas_call | solution.py:57
  106.4 3.4 %all-to-all-start.1 = ((bf16[8,20,320]{2,1,0:T(8,128)(2,1)}), bf16[8,20,320]{2,1,0:T(8,128)(2,1)S(1)}, u32[]{:S(2)}, u32[]{:S(2)}) async-start(bf16[8,20,320]{2,1,0:T(8,128)(2,1)} %shard_map.102), calls=%async_computation.1 | async-start | bytes 294912 | tf_op jit(solution)/shard_map/all_to_all | solution.py:561
  109.8 1.4 %shard_map.105 = (bf16[320,384]{1,0:T(8,128)(2,1)}, bf16[320,384]{1,0:T(8,128)(2,1)}) custom-call(s32[5]{0:T(128)S(1)} %stack.23.place, f32[2,320,384]{2,1,0:T(8,128)S(1)} %get-tuple-element.102.mine, bf16[2,320,384]{2,1,0:T(8,128)(2,1)S(1)} %collective-permute-done.14.got), custom_call_target="tpu_custom_call" | custom-call | tf_op jit(solution)/shard_map/pallas_call | solution.py:57
  111.2 5.2 %all-to-all-done.1.final = bf16[8,20,320]{2,1,0:T(8,128)(2,1)S(1)} async-done(((bf16[8,20,320]{2,1,0:T(8,128)(2,1)}), bf16[8,20,320]{2,1,0:T(8,128)(2,1)S(1)}, u32[]{:S(2)}, u32[]{:S(2)}) %all-to-all-start.1) | async-done | bytes 102432 | tf_op jit(solution)/shard_map/all_to_all | solution.py:561
  116.4 1.3 %shard_map.106 = (f32[3,20,320]{2,1,0:T(8,128)}, f32[20,320]{1,0:T(8,128)}) custom-call(s32[5]{0:T(128)S(1)} %stack.23.place, bf16[8,20,320]{2,1,0:T(8,128)(2,1)S(1)} %all-to-all-done.1.final), custom_call_target="tpu_custom_call" | custom-call | tf_op jit(solution)/shard_map/pallas_call | solution.py:57
  (24 shorter events, 2.4 us)
Async XLA Ops:
  7.2 13.4 %copy-start = (bf16[384,1280]{1,0:T(8,128)(2,1)S(1)}, bf16[384,1280]{1,0:T(8,128)(2,1)}, u32[]{:S(2)}) copy-start(bf16[384,1280]{1,0:T(8,128)(2,1)} %cotangent.2) | copy-start | bytes 2949124
  7.2 13.4 %copy-start.1 = (bf16[320,1280]{1,0:T(8,128)(2,1)S(1)}, bf16[320,1280]{1,0:T(8,128)(2,1)}, u32[]{:S(2)}) copy-start(bf16[320,1280]{1,0:T(8,128)(2,1)} %w_out.3) | copy-start | bytes 2457604
  7.2 67.7 %all-gather.3.cloned.1.call-start = ((), (), s32[]{:S(2)}) async-start(), calls=%async_computation.2 | async-start | bytes 8847360 | tf_op jit(solution)/shard_map/all_gather | solution.py:514
  14.8 8.3 %collective-permute-start = (bf16[256,384]{1,0:T(8,128)(2,1)}, bf16[256,384]{1,0:T(8,128)(2,1)S(1)}, u32[]{:S(2)}, u32[]{:S(2)}) collective-permute-start(bf16[256,384]{1,0:T(8,128)(2,1)} %get-tuple-element.60), channel_id=1, source_target_pairs={{0,4},{4,8},{8,12},{12,0},{1,5},{5,9},{9,13},{13,1},{2,6},{6,10},{... | collective-permute-start | bytes 589832 | tf_op jit(solution)/shard_map/ppermute | solution.py:39
  16.4 11.8 %collective-permute-start.1 = (bf16[256,384]{1,0:T(8,128)(2,1)}, bf16[256,384]{1,0:T(8,128)(2,1)S(1)}, u32[]{:S(2)}, u32[]{:S(2)}) collective-permute-start(bf16[256,384]{1,0:T(8,128)(2,1)} %get-tuple-element.61), channel_id=1, source_target_pairs={{0,8},{4,12},{8,0},{12,4},{1,9},{5,13},{9,1},{13,5},{2,10},{6,14},... | collective-permute-start | bytes 589832 | tf_op jit(solution)/shard_map/ppermute | solution.py:39
  19.1 9.0 %collective-permute-start.2 = (bf16[256,384]{1,0:T(8,128)(2,1)}, bf16[256,384]{1,0:T(8,128)(2,1)S(1)}, u32[]{:S(2)}, u32[]{:S(2)}) collective-permute-start(bf16[256,384]{1,0:T(8,128)(2,1)} %get-tuple-element.62), channel_id=1, source_target_pairs={{0,12},{4,0},{8,4},{12,8},{1,13},{5,1},{9,5},{13,9},{2,14},{6,2},{... | collective-permute-start | bytes 589832 | tf_op jit(solution)/shard_map/ppermute | solution.py:39
  28.8 21.0 %collective-permute-start.6 = (bf16[176,1152]{1,0:T(8,128)(2,1)S(1)}, bf16[176,1152]{1,0:T(8,128)(2,1)S(1)}, u32[]{:S(2)}, u32[]{:S(2)}) collective-permute-start(bf16[176,1152]{1,0:T(8,128)(2,1)S(1)} %get-tuple-element.80), channel_id=1, source_target_pairs={{0,16},{16,32},{32,48},{48,64},{64,80},{80,96},{96,112},{112,128},... | collective-permute-start | bytes 1216520 | tf_op jit(solution)/shard_map/ppermute | solution.py:39
  30.8 19.0 %collective-permute-start.7 = (bf16[176,1152]{1,0:T(8,128)(2,1)S(1)}, bf16[176,1152]{1,0:T(8,128)(2,1)S(1)}, u32[]{:S(2)}, u32[]{:S(2)}) collective-permute-start(bf16[176,1152]{1,0:T(8,128)(2,1)S(1)} %get-tuple-element.81), channel_id=1, source_target_pairs={{0,240},{16,0},{32,16},{48,32},{64,48},{80,64},{96,80},{112,96},{1... | collective-permute-start | bytes 1216520 | tf_op jit(solution)/shard_map/ppermute | solution.py:39
  37.9 11.9 %collective-permute-start.3 = (bf16[80,384]{1,0:T(8,128)(2,1)S(1)}, bf16[80,384]{1,0:T(8,128)(2,1)S(1)}, u32[]{:S(2)}, u32[]{:S(2)}) collective-permute-start(bf16[80,384]{1,0:T(8,128)(2,1)S(1)} %get-tuple-element.70), channel_id=1, source_target_pairs={{0,4},{4,8},{8,12},{12,0},{1,5},{5,9},{9,13},{13,1},{2,6},{6,10},{... | collective-permute-start | bytes 184328 | tf_op jit(solution)/shard_map/ppermute | solution.py:39
  39.3 10.5 %collective-permute-start.4 = (bf16[80,384]{1,0:T(8,128)(2,1)S(1)}, bf16[80,384]{1,0:T(8,128)(2,1)S(1)}, u32[]{:S(2)}, u32[]{:S(2)}) collective-permute-start(bf16[80,384]{1,0:T(8,128)(2,1)S(1)} %get-tuple-element.71), channel_id=1, source_target_pairs={{0,8},{4,12},{8,0},{12,4},{1,9},{5,13},{9,1},{13,5},{2,10},{6,14},... | collective-permute-start | bytes 184328 | tf_op jit(solution)/shard_map/ppermute | solution.py:39
  41.9 7.9 %collective-permute-start.5 = (bf16[80,384]{1,0:T(8,128)(2,1)S(1)}, bf16[80,384]{1,0:T(8,128)(2,1)S(1)}, u32[]{:S(2)}, u32[]{:S(2)}) collective-permute-start(bf16[80,384]{1,0:T(8,128)(2,1)S(1)} %get-tuple-element.72), channel_id=1, source_target_pairs={{0,12},{4,0},{8,4},{12,8},{1,13},{5,1},{9,5},{13,9},{2,14},{6,2},{... | collective-permute-start | bytes 184328 | tf_op jit(solution)/shard_map/ppermute | solution.py:39
  57.8 7.8 %collective-permute-start.8 = (bf16[160,1152]{1,0:T(8,128)(2,1)S(1)}, bf16[160,1152]{1,0:T(8,128)(2,1)S(1)}, u32[]{:S(2)}, u32[]{:S(2)}) collective-permute-start(bf16[160,1152]{1,0:T(8,128)(2,1)S(1)} %get-tuple-element.91), channel_id=1, source_target_pairs={{0,240},{16,0},{32,16},{48,32},{64,48},{80,64},{96,80},{112,96},{1... | collective-permute-start | bytes 1105928 | tf_op jit(solution)/shard_map/ppermute | solution.py:39
  60.0 9.6 %collective-permute-start.9 = (bf16[160,1152]{1,0:T(8,128)(2,1)S(1)}, bf16[160,1152]{1,0:T(8,128)(2,1)S(1)}, u32[]{:S(2)}, u32[]{:S(2)}) collective-permute-start(bf16[160,1152]{1,0:T(8,128)(2,1)S(1)} %get-tuple-element.92), channel_id=1, source_target_pairs={{0,16},{16,32},{32,48},{48,64},{64,80},{80,96},{96,112},{112,128},... | collective-permute-start | bytes 1105928 | tf_op jit(solution)/shard_map/ppermute | solution.py:39
  71.1 13.5 %collective-permute-start.10 = (bf16[320,384]{1,0:T(8,128)(2,1)S(1)}, bf16[320,384]{1,0:T(8,128)(2,1)S(1)}, u32[]{:S(2)}, u32[]{:S(2)}) collective-permute-start(bf16[320,384]{1,0:T(8,128)(2,1)S(1)} %get-tuple-element.97), channel_id=1, source_target_pairs={{0,4},{4,8},{8,12},{12,0},{1,5},{5,9},{9,13},{13,1},{2,6},{6,10},{... | collective-permute-start | bytes 737288 | tf_op jit(solution)/shard_map/ppermute | solution.py:39
  71.3 13.4 %collective-permute-start.11 = (bf16[320,384]{1,0:T(8,128)(2,1)S(1)}, bf16[320,384]{1,0:T(8,128)(2,1)S(1)}, u32[]{:S(2)}, u32[]{:S(2)}) collective-permute-start(bf16[320,384]{1,0:T(8,128)(2,1)S(1)} %get-tuple-element.98), channel_id=1, source_target_pairs={{0,8},{4,12},{8,0},{12,4},{1,9},{5,13},{9,1},{13,5},{2,10},{6,14},... | collective-permute-start | bytes 737288 | tf_op jit(solution)/shard_map/ppermute | solution.py:39
  74.2 10.6 %collective-permute-start.12 = (bf16[320,384]{1,0:T(8,128)(2,1)S(1)}, bf16[320,384]{1,0:T(8,128)(2,1)S(1)}, u32[]{:S(2)}, u32[]{:S(2)}) collective-permute-start(bf16[320,384]{1,0:T(8,128)(2,1)S(1)} %get-tuple-element.99), channel_id=1, source_target_pairs={{0,12},{4,0},{8,4},{12,8},{1,13},{5,1},{9,5},{13,9},{2,14},{6,2},{... | collective-permute-start | bytes 737288 | tf_op jit(solution)/shard_map/ppermute | solution.py:39
  81.1 23.9 %all-to-all-start = ((bf16[8,208,256]{2,1,0:T(8,128)(2,1)}), bf16[8,208,256]{2,1,0:T(8,128)(2,1)S(1)}, u32[]{:S(2)}, u32[]{:S(2)}) async-start(bf16[8,208,256]{2,1,0:T(8,128)(2,1)} %shard_map.101), calls=%async_computation | async-start | bytes 1703936 | tf_op jit(solution)/shard_map/all_to_all | solution.py:557
  89.5 2.7 %collective-permute-start.13 = (bf16[2,2,320,384]{3,2,1,0:T(8,128)(2,1)S(1)}, bf16[2,2,320,384]{3,2,1,0:T(8,128)(2,1)S(1)}, u32[]{:S(2)}, u32[]{:S(2)}) collective-permute-start(bf16[2,2,320,384]{3,2,1,0:T(8,128)(2,1)S(1)} %get-tuple-element.101), channel_id=1, source_target_pairs={{0,1},{1,0},{2,3},{3,2},{4,5},{5,4},{6,7},{7,6},{8,9},{9,8},{10,11... | collective-permute-start | bytes 2949128 | tf_op jit(solution)/shard_map/ppermute | solution.py:39
  92.8 17.0 %collective-permute-start.14 = (bf16[2,320,384]{2,1,0:T(8,128)(2,1)S(1)}, bf16[2,320,384]{2,1,0:T(8,128)(2,1)S(1)}, u32[]{:S(2)}, u32[]{:S(2)}) collective-permute-start(bf16[2,320,384]{2,1,0:T(8,128)(2,1)S(1)} %get-tuple-element.103), channel_id=1, source_target_pairs={{0,2},{2,0},{1,3},{3,1},{4,6},{6,4},{5,7},{7,5},{8,10},{10,8},{9,1... | collective-permute-start | bytes 1474568 | tf_op jit(solution)/shard_map/ppermute | solution.py:39
  106.4 10.0 %all-to-all-start.1 = ((bf16[8,20,320]{2,1,0:T(8,128)(2,1)}), bf16[8,20,320]{2,1,0:T(8,128)(2,1)S(1)}, u32[]{:S(2)}, u32[]{:S(2)}) async-start(bf16[8,20,320]{2,1,0:T(8,128)(2,1)} %shard_map.102), calls=%async_computation.1 | async-start | bytes 294912 | tf_op jit(solution)/shard_map/all_to_all | solution.py:561
Sparse Core Ops, SparseCore 0:
  10.1 55.4 all-gather.2
